TPU v7x, 256 devices: a whole 4x4x8 slice. The times are simulated.
256 devices in a mesh: frame: 32 (over z, x), pos: 8 (over y, core).
Axes of the slice: x: 4, y: 4, z: 8, core: 2. Of those that a mesh axis runs over, the one named last changes fastest.
Arguments:
- qkv: bfloat16 [3, 32, 1536, 3072], P(None, 'frame', 'pos'), may hold values from -24 to 24
- head_kind: int32 [24], replicated, may hold values from 0 to 1, as said below
- out_weight: bfloat16 [3072, 3072], P(('frame', 'pos')), may hold values from -0.109375 to 0.109375
Outputs:
- projected: bfloat16 [32, 1536, 3072], P('frame', 'pos')
Inputs may be any that keep to these rules, and one draw needn't show every extreme that they name: `head_kind`: exactly 16 entries are 0 and 8 entries are 1.
All inputs are finite; a program needn't handle non-finite values.
Results may differ from a plain program's by a relative error of at most 0.0065.
Values may be sent and summed in bfloat16 or wider, within the bound.
No kernel may reach another device: no remote copies, remote signals or barrier semaphores. Data moves between devices by JAX's collectives and lax.ppermute only.
A program may use at most 128 MiB of HBM per device.

v0:
```python
import jax
import jax.numpy as jnp
from jax import lax
from jax.sharding import PartitionSpec as P

HEADS = 24
HEAD_SIZE = 128
SPATIAL = 16
D = 3072


def head_selector(head_kind):
    spatial_flag = 1 - head_kind
    head_rank = jnp.where(
        head_kind == 0, jnp.cumsum(spatial_flag) - 1, SPATIAL + jnp.cumsum(head_kind) - 1
    )
    return (head_rank[None, :] == jnp.arange(HEADS)[:, None]).astype(jnp.bfloat16)


def temporal_block(stacked):
    score_matrix = jnp.einsum(
        "fphd,gphd->phfg", stacked[0], stacked[1], preferred_element_type=jnp.float32
    ) * HEAD_SIZE ** (-0.5)
    top_score = jnp.max(score_matrix, axis=-1, keepdims=True)
    expon = jnp.exp(score_matrix - top_score)
    totals = jnp.sum(expon, axis=-1)
    summed_values = jnp.einsum(
        "phfg,gphd->fphd",
        expon.astype(jnp.bfloat16),
        stacked[2],
        preferred_element_type=jnp.float32,
    )
    result = (summed_values / jnp.transpose(totals, (2, 0, 1))[..., None]).astype(jnp.bfloat16)
    return lax.all_to_all(result, "frame", split_axis=0, concat_axis=1, tiled=True)


def shards(qkv, head_kind, out_weight):
    frames_here = qkv.shape[1]
    places_here = qkv.shape[2]
    selector = head_selector(head_kind)
    stacked = qkv.reshape(3, frames_here, places_here, HEADS, HEAD_SIZE)
    grouped = jnp.einsum(
        "cfphd,rh->cfprd", stacked, selector, preferred_element_type=jnp.float32
    ).astype(jnp.bfloat16)
    spatial_part = grouped[:, :, :, :SPATIAL]
    temporal_part = grouped[:, :, :, SPATIAL:]
    temporal_out = temporal_block(
        lax.all_to_all(temporal_part, "frame", split_axis=2, concat_axis=1, tiled=True)
    )
    query_matrix = spatial_part[0]
    start_max = jnp.full((frames_here, SPATIAL, places_here), -1e30, jnp.float32)
    score_matrix = jnp.einsum(
        "fqhd,fkhd->fhqk",
        query_matrix,
        lax.all_gather(spatial_part[1], "pos", axis=1, tiled=True),
        preferred_element_type=jnp.float32,
    ) * HEAD_SIZE ** (-0.5)
    new_max = jnp.maximum(start_max, jnp.max(score_matrix, axis=-1))
    expon = jnp.exp(score_matrix - new_max[..., None])
    new_sum = jnp.sum(expon, axis=-1)
    added = jnp.einsum(
        "fhqk,fkhd->fhqd",
        expon.astype(jnp.bfloat16),
        lax.all_gather(spatial_part[2], "pos", axis=1, tiled=True),
        preferred_element_type=jnp.float32,
    )
    spatial_out = jnp.transpose((added / new_sum[..., None]).astype(jnp.bfloat16), (0, 2, 1, 3))
    combined = jnp.concatenate([spatial_out, temporal_out], axis=2)
    head_outputs = jnp.einsum(
        "fprd,rh->fphd", combined, selector, preferred_element_type=jnp.float32
    ).astype(jnp.bfloat16)
    flat_outputs = head_outputs.reshape(frames_here * places_here, D)
    summed_values = jnp.dot(
        flat_outputs,
        lax.all_gather(out_weight, ("frame", "pos"), axis=0, tiled=True),
        preferred_element_type=jnp.float32,
    )
    return summed_values.astype(jnp.bfloat16).reshape(frames_here, places_here, D)


def solution(mesh):
    placed = (P(None, "frame", "pos", None), P(), P(("frame", "pos"), None))
    return jax.shard_map(
        shards, mesh=mesh, in_specs=placed, out_specs=P("frame", "pos", None), check_vma=False
    )
```

profile of v0, /device:TPU:2, one launch (start us, length us, event | category | flops | bytes accessed | tf_op | source)
XLA Modules:
  0.0 290.1 jit_solution(13362293934394035903)
XLA Ops:
  6.5 0.0 copy-start.1
  6.5 0.0 all-gather.7.cloned.1.call-start
  6.5 0.7 subtract_bitcast_fusion
  7.3 0.1 copy.42
  7.4 0.7 copy.43
  8.2 3.0 %copy.67 = bf16[72,8,24,128]{3,2,1,0:T(8,128)(2,1)S(1)} copy(bf16[72,8,24,128]{3,1,2,0:T(8,128)(2,1)} %bitcast.78) | data formatting | bytes 7077888
  11.2 0.1 add_reduce_fusion
  11.3 0.0 copy-done.1
  11.3 1.2 convert_bitcast_fusion
  12.5 1.6 slice_bitcast_fusion.2
  14.1 0.0 all-gather.7.cloned.1.call-update
  14.2 0.0 all-gather.9.cloned.1.call-start
  14.2 0.7 all-gather.9.cloned.1.call-update
  14.9 0.0 all-gather.11.cloned.1.call-start
  15.0 0.7 all-gather.11.cloned.1.call-update
  15.7 0.2 slice.39
  15.9 0.2 copy.50
  16.1 0.0 copy-start
  16.1 42.6 %all_to_all.21 = bf16[3,1,192,8,128]{4,3,0,1,2:T(8,128)(2,1)S(1)} all-to-all(bf16[3,1,192,8,128]{4,3,0,1,2:T(8,128)(2,1)S(1)} %copy.50), channel_id=1, replica_groups=mesh['frame'=32,'pos'=8] {'frame'}, dimensions={2} | all-to-all | bytes 2359296 | tf_op jit(solution)/shard_map/all_to_all | solution.py:48
  58.7 0.2 fusion.45
  59.0 0.3 fusion.46
  59.3 0.2 fusion.31
  59.5 0.4 fusion.17
  59.9 0.2 copy.58
  60.1 18.4 %all_to_all.22 = bf16[32,6,8,128]{3,2,1,0:T(8,128)(2,1)S(1)} all-to-all(bf16[32,6,8,128]{3,2,1,0:T(8,128)(2,1)S(1)} %copy.58), channel_id=1, replica_groups=mesh['frame'=32,'pos'=8] {'frame'}, dimensions={0} | all-to-all | bytes 786432 | tf_op jit(solution)/shard_map/all_to_all | solution.py:34
  78.5 0.1 copy.59
  78.5 0.0 all-gather.7.cloned.1.call-done
  78.6 0.0 copy-done
  78.6 13.8 %multiply_reduce_fusion = (f32[16,192]{1,0:T(8,128)S(1)}, f32[16,192,1536]{2,1,0:T(8,128)}) fusion(bf16[1,1,1536,16,128]{4,3,1,0,2:T(8,128)(2,1)} %all-gather.7.cloned.1.call-done, bf16[192,16,128]{2,1,0:T(8,128)(2,1)S(1)} %copy-done), kind=kOutput, calls=%fused_computation.1 | convolution fusion | flops 1217393664 | bytes 25964544 | tf_op jit(solution)/shard_map/fqhd,fkhd->fhqk/dot_general | solution.py:52
  92.4 10.0 %fusion = f32[16,192]{1,0:T(8,128)S(1)} fusion(f32[16,192,1536]{2,1,0:T(8,128)} %get-tuple-element.14, f32[16,192]{1,0:T(8,128)S(1)} %broadcast_maximum_fusion), kind=kLoop, calls=%fused_computation.2 | loop fusion | flops 14152704 | bytes 18898944 | tf_op jit(solution)/shard_map/reduce_sum | solution.py:60
  102.5 3.7 %all-gather.9.cloned.1.call-done = bf16[1,1,1536,16,128]{4,3,1,0,2:T(8,128)(2,1)} async-done(((bf16[1,1,192,16,128]{4,3,1,0,2:T(8,128)(2,1)}), bf16[1,1,1536,16,128]{4,3,1,0,2:T(8,128)(2,1)}) %all-gather.9.cloned.1.call-update) | async-done | bytes 6291472 | tf_op jit(solution)/shard_map/all_gather | solution.py:64
  106.2 14.2 %fusion.25 = bf16[1,192,16,128]{3,1,2,0:T(8,128)(2,1)S(1)} fusion(bf16[1,1,1536,16,128]{4,3,1,0,2:T(8,128)(2,1)} %all-gather.9.cloned.1.call-done, f32[16,192,1536]{2,1,0:T(8,128)} %get-tuple-element.14, f32[16,192]{1,0:T(8,128)S(1)} %broadcast_maximum_fusion, f32[16,192]{1,0:T(8,128)S(1)} %fusion), kind=kOutput, calls=%fused_computation.27 | convolution fusion | flops 1222901760 | bytes 25976832 | tf_op jit(solution)/shard_map/fhqk,fkhd->fhqd/dot_general | solution.py:61
  120.4 0.1 maximum_bitcast_fusion
  120.5 1.0 convolution_convert_fusion.1
  121.5 126.5 %all-gather.11.cloned.1.call-done = bf16[256,12,3072]{2,1,0:T(8,128)(2,1)} async-done(((bf16[1,12,3072]{2,1,0:T(8,128)(2,1)}), bf16[256,12,3072]{2,1,0:T(8,128)(2,1)}) %all-gather.11.cloned.1.call-update) | async-done | bytes 18874384 | tf_op jit(solution)/shard_map/all_gather | solution.py:75
  248.0 26.0 %reshape.135 = bf16[3072,3072]{1,0:T(8,128)(2,1)} reshape(bf16[256,12,3072]{2,1,0:T(8,128)(2,1)} %all-gather.11.cloned.1.call-done) | data formatting | bytes 37748736
  274.1 9.5 %fusion.11 = bf16[1,192,3072]{2,1,0:T(8,128)(2,1)} fusion(bf16[3072,3072]{1,0:T(8,128)(2,1)} %reshape.135, bf16[24,8,24,128]{3,2,1,0:T(8,128)(2,1)S(1)} %bitcast.82), kind=kOutput, calls=%fused_computation.13 | convolution fusion | flops 3624468480 | bytes 21233664 | tf_op jit(solution)/shard_map/dot_general | solution.py:73
  (4 shorter events, 0.1 us)
Async XLA Ops:
  6.5 4.8 %copy-start.1 = (s32[24]{0:T(128)S(1)}, s32[24]{0:T(128)}, u32[]{:S(2)}) copy-start(s32[24]{0:T(128)} %param.4) | copy-start | bytes 292
  6.5 72.0 %all-gather.7.cloned.1.call-start = ((), (), s32[]{:S(2)}) async-start(), calls=%async_computation.2 | async-start | bytes 7077888 | tf_op jit(solution)/shard_map/all_gather | solution.py:55
  14.2 92.0 %all-gather.9.cloned.1.call-start = ((), (), s32[]{:S(2)}) async-start(), calls=%async_computation.3 | async-start | bytes 7077888 | tf_op jit(solution)/shard_map/all_gather | solution.py:64
  14.9 233.1 %all-gather.11.cloned.1.call-start = ((), (), s32[]{:S(2)}) async-start(), calls=%async_computation.4 | async-start | bytes 25264128 | tf_op jit(solution)/shard_map/all_gather | solution.py:75
  16.1 62.5 %copy-start = (bf16[192,16,128]{2,1,0:T(8,128)(2,1)S(1)}, bf16[192,16,128]{2,1,0:T(8,128)(2,1)}, u32[]{:S(2)}) copy-start(bf16[192,16,128]{2,1,0:T(8,128)(2,1)} %get-tuple-element.5) | copy-start | bytes 2359300
Sparse Core Ops, SparseCore 0:
  14.3 46.4 all-gather.6
  62.6 43.5 all-gather.8
  110.1 137.9 all-gather.10
where the time goes:
time: 292 us; the launch traced here: 290 us
  waiting for transfers between devices  132 us (45%)
  blocking collectives  61 us (21%)
  matrix products  40.6 us (14%)
  local copies, waits for them, and re-layouts  32.3 us (11%)
  between operations  13.2 us (5%)
  other arithmetic  11.3 us (4%)
    all_gather x1, waiting for transfers between devices, shards(): lax.all_gather(out_weight, ('frame', 'pos'), axis=0, tiled=True)  126 us
    all_to_all x1, blocking collectives, shards(): lax.all_to_all(temporal_part, 'frame', split_axis=2, concat_axis=1, tiled...  42.6 us
    unnamed x6, local copies, waits for them, and re-layouts  29.1 us
    all_to_all x1, blocking collectives, temporal_block(): lax.all_to_all(result, 'frame', split_axis=0, concat_axis=1, tiled=True)  18.4 us
    dot_general x1, matrix products, shards(): jnp.einsum('fhqk,fkhd->fhqd', expon.astype(jnp.bfloat16), lax.all_gather(...  14.2 us
    dot_general x1, matrix products, shards(): jnp.einsum('fqhd,fkhd->fhqk', query_matrix, lax.all_gather(spatial_part[1...  13.8 us
    reduce_sum x1, other arithmetic, shards(): new_sum = jnp.sum(expon, axis=-1)  10 us
    dot_general x1, matrix products, shards(): jnp.dot(flat_outputs, lax.all_gather(out_weight, ('frame', 'pos'), axis=0...  9.52 us
  transfers between devices with their start and end apart: 3, of which 2 were waited for; matrix products, arithmetic and copies ran while one was open for 14% of the time, Pallas kernels for 0%

commit v1 on v0

v1 whole, which is shorter than its diff:
```python
import jax
import jax.numpy as jnp
from jax import lax
from jax.experimental import pallas as pl
from jax.experimental.pallas import tpu as pltpu
from jax.sharding import Mesh, PartitionSpec as P

HEADS = 24
SIZE = 128
SPATIAL = 16
D = 3072
FRAMES = 32
ROWS = 192
RING = 4
SHARE = D // RING
GROUP = 48
EXP_SCALE = 1.4426950408889634 * SIZE ** -0.5
POS = ("y", "core")
BF16 = jnp.bfloat16
F32 = jnp.float32
VMEM = pl.BlockSpec(memory_space=pltpu.VMEM)
SMEM = pl.BlockSpec(memory_space=pltpu.SMEM)
ANY = pl.BlockSpec(memory_space=pl.ANY)


def shape(*dims, dtype=BF16):
    return jax.ShapeDtypeStruct(dims, dtype)


def params():
    return pltpu.CompilerParams(vmem_limit_bytes=56 * 1024 * 1024)


def cost(flops, nbytes, exps=0):
    return pl.CostEstimate(flops=flops, bytes_accessed=nbytes, transcendentals=exps)


def pack_kernel(ids, place, qkv, *outs):
    y, core = place[0], place[1]
    for part in range(2):
        for step in range(RING):
            to = ((y + step) % RING) * 2 + (core + part) % 2
            for head in range(2):
                column = pl.multiple_of(ids[to * 2 + head] * SIZE, SIZE)
                outs[part * RING + step][:, head] = qkv[:, :, pl.ds(column, SIZE)]
    temporal = outs[8]
    for head in range(HEADS - SPATIAL):
        column = pl.multiple_of(ids[SPATIAL + head] * SIZE, SIZE)
        for piece in range(ROWS // GROUP):
            rows = slice(piece * GROUP, (piece + 1) * GROUP)
            temporal[head * 4 + piece] = qkv[:, rows, pl.ds(column, SIZE)]


def pack(ids, place, qkv):
    outs = [shape(3, 2, ROWS, SIZE)] * 8 + [shape(FRAMES, 3, GROUP, SIZE)]
    return pl.pallas_call(
        pack_kernel,
        out_shape=outs,
        in_specs=[SMEM, SMEM, VMEM],
        out_specs=[VMEM] * 9,
        compiler_params=params(),
        cost_estimate=cost(0, 7_000_000),
        name="pack",
    )(ids, place, qkv)


def attend(query, key, value_ones, keep=None):
    score = lax.dot_general(query, key, (((1,), (1,)), ((), ())), preferred_element_type=F32)
    if keep is not None:
        score = jnp.where(keep, score, -1e30)
    top = jnp.max(score, axis=1, keepdims=True)
    weight = jnp.exp2((score - top) * EXP_SCALE).astype(BF16)
    both = jnp.dot(weight, value_ones, preferred_element_type=F32)
    return (both[:, :SIZE] / both[:, SIZE:]).astype(BF16)


def spatial_kernel(place, *refs):
    chunks, outs = refs[:8], refs[8:]
    y = place[0]
    ones = jnp.ones((8 * ROWS, SIZE), BF16)
    for head in range(2):
        key = jnp.concatenate([chunk[1, head] for chunk in chunks], axis=0)
        value = jnp.concatenate([chunk[2, head] for chunk in chunks], axis=0)
        value_ones = jnp.concatenate([value, ones], axis=1)
        for pair in range(4):
            two = (pair * 2, pair * 2 + 1)
            query = jnp.concatenate([chunks[i][0, head] for i in two], axis=0)
            result = attend(query, key, value_ones)
            for n, i in enumerate(two):
                origin = (y + RING - i % RING) % RING
                outs[i // RING][origin, :, head * SIZE : (head + 1) * SIZE] = result[
                    n * ROWS : (n + 1) * ROWS
                ]


def spatial(place, chunks):
    return pl.pallas_call(
        spatial_kernel,
        out_shape=[shape(RING, ROWS, 2 * SIZE)] * 2,
        in_specs=[SMEM] + [VMEM] * 8,
        out_specs=[VMEM] * 2,
        compiler_params=params(),
        cost_estimate=cost(4_800_000_000, 4_000_000, 4_700_000),
        name="spatial",
    )(place, *chunks)


def temporal_kernel(heads, out):
    span = 16
    count = FRAMES * span
    same = lax.broadcasted_iota(jnp.int32, (count, count), 0) % span == (
        lax.broadcasted_iota(jnp.int32, (count, count), 1) % span
    )
    ones = jnp.ones((count, SIZE), BF16)
    for piece in range(GROUP // span):
        rows = slice(piece * span, (piece + 1) * span)
        query, key, value = (heads[:, c, rows].reshape(count, SIZE) for c in range(3))
        result = attend(query, key, jnp.concatenate([value, ones], axis=1), same)
        out[:, rows] = result.reshape(FRAMES, span, SIZE)


def temporal(heads):
    return pl.pallas_call(
        temporal_kernel,
        out_shape=shape(FRAMES, GROUP, SIZE),
        in_specs=[VMEM],
        out_specs=VMEM,
        compiler_params=params(),
        cost_estimate=cost(600_000_000, 1_600_000, 800_000),
        name="temporal",
    )(heads)


def project_kernel(ids, place, weight, *refs):
    spatial_in = refs[:8]
    temporal_in = (refs[8], refs[9], None, refs[12])
    out, held, tokens, sems = refs[13:]
    y, core = place[0], place[1]
    copies = []
    ranks = []
    for step in range(RING):
        origin = (y + RING - step) % RING
        for part in range(2):
            first = origin * 4 + ((core + part) % 2) * 2
            ranks += [first, first + 1]
    ranks += [SPATIAL + head for head in range(HEADS - SPATIAL)]
    for slot, rank in enumerate(ranks):
        start = pl.multiple_of(ids[rank] * SIZE, SIZE)
        copy = pltpu.make_async_copy(
            weight.at[pl.ds(start, SIZE)], held.at[pl.ds(slot * SIZE, SIZE)], sems.at[slot]
        )
        copy.start()
        copies.append(copy)
    for slot, block in enumerate(spatial_in):
        tokens[:, :, slot * 256 : (slot + 1) * 256] = block[...]
    for step in range(RING):
        origin = (y + RING - step) % RING
        for head in range(HEADS - SPATIAL):
            if step == 2:
                half = (refs[10], refs[11])[head // 4]
                rows = half[(head % 4) * 4 : (head % 4) * 4 + 4]
            else:
                whole = temporal_in[step]
                rows = whole[head * 4 : head * 4 + 4]
            lanes = slice((SPATIAL + head) * SIZE, (SPATIAL + head + 1) * SIZE)
            tokens[origin, :, lanes] = rows.reshape(ROWS, SIZE)
    for copy in copies:
        copy.wait()
    left = tokens[...].reshape(RING * ROWS, D)
    for n in range(SHARE // 256):
        columns = slice(n * 256, (n + 1) * 256)
        total = jnp.dot(left, held[:, columns], preferred_element_type=F32)
        out[:, :, columns] = total.astype(BF16).reshape(RING, ROWS, 256)


def project(ids, place, weight, spatial_in, temporal_in):
    return pl.pallas_call(
        project_kernel,
        out_shape=shape(RING, ROWS, SHARE),
        in_specs=[SMEM, SMEM, ANY] + [VMEM] * 13,
        out_specs=VMEM,
        scratch_shapes=[
            pltpu.VMEM((D, SHARE), BF16),
            pltpu.VMEM((RING, ROWS, D), BF16),
            pltpu.SemaphoreType.DMA((HEADS,)),
        ],
        compiler_params=params(),
        cost_estimate=cost(3_600_000_000, 11_000_000),
        name="project",
    )(ids, place, weight, *spatial_in, *temporal_in)


def hop(array, steps, part=0):
    perm = [
        (y * 2 + core, ((y + steps) % RING) * 2 + (core + part) % 2)
        for y in range(RING)
        for core in range(2)
    ]
    return lax.ppermute(array, POS, perm)


def weight_share(out_weight):
    here = jnp.transpose(out_weight.reshape(12, RING, SHARE), (1, 0, 2))
    sent = jnp.broadcast_to(here[:, None], (RING, 2, 12, SHARE)).reshape(8, 12, SHARE)
    rows = lax.all_to_all(sent, POS, 0, 0, tiled=True).reshape(96, SHARE)
    own = lax.dynamic_slice_in_dim(rows, lax.axis_index("core") * 48, 48, 0)
    gathered = lax.all_gather(own, ("frame", "core"), axis=0, tiled=False)
    return gathered.reshape(D, SHARE)


def shards(qkv, head_kind, out_weight):
    y = lax.axis_index("y")
    core = lax.axis_index("core")
    place = jnp.stack([y, core]).astype(jnp.int32)
    ids = jnp.argsort(head_kind, stable=True).astype(jnp.int32)
    weight = weight_share(out_weight)

    packed = pack(ids, place, qkv.reshape(3, ROWS, D))
    chunks = [packed[0]]
    for i in range(1, 8):
        chunks.append(hop(packed[i], i % RING, i // RING))
    across = lax.all_to_all(packed[8], "frame", 0, 0, tiled=True)
    mine, other = spatial(place, chunks)
    theirs = hop(other, 0, 1)
    mine_behind, mine_ahead = hop(mine, 1), hop(mine, -1)
    theirs_behind, theirs_ahead = hop(theirs, 1), hop(theirs, -1)
    mine_far = hop(mine_behind, 1)
    theirs_far = hop(theirs_ahead, -1)

    back = lax.all_to_all(temporal(across), "frame", 0, 0, tiled=True)
    back_behind, back_ahead = hop(back, 1), hop(back, -1)
    far_low = hop(back_behind[:16], 1)
    far_high = hop(back_ahead[16:], -1)

    out = project(
        ids,
        place,
        weight,
        [mine, theirs, mine_behind, theirs_behind, mine_far, theirs_far, mine_ahead, theirs_ahead],
        [back, back_behind, far_low, far_high, back_ahead],
    )
    whole = lax.all_to_all(out, "y", 0, 0, tiled=True)
    return jnp.transpose(whole, (1, 0, 2)).reshape(1, ROWS, D)


def solution(mesh):
    frames, positions = mesh.devices.shape
    split = Mesh(
        mesh.devices.reshape(frames, positions // 2, 2), ("frame", "y", "core")
    )
    placed = (P(None, "frame", POS, None), P(), P(("frame", "y", "core"), None))
    return jax.shard_map(
        shards, mesh=split, in_specs=placed, out_specs=P("frame", POS, None), check_vma=False
    )
```

time: 292 us -> 174 us (0.60)
  waiting for transfers between devices: 132 us -> 67.3 us
  blocking collectives: 61 us -> 20 us
  matrix products: 40.6 us -> 0 us
  starting transfers between devices: 0.08 us -> 36.7 us
  Pallas kernels: 0 us -> 26.2 us
  local copies, waits for them, and re-layouts: 32.3 us -> 7.52 us
  other arithmetic: 11.3 us -> 2.28 us
    all_gather x3 -> x1, waiting for transfers between devices: 130 us -> 0.01 us  [weight_share(): gathered = lax.all_gather(own, ('frame', 'core'), axis=0, tiled=False)]
    all_to_all x2 -> x1, blocking collectives: 61 us -> 20 us  [shards(): whole = lax.all_to_all(out, 'y', 0, 0, tiled=True)]
    dot_general x7 -> x0, matrix products: 40.6 us -> none  [the longest x1 14.2 us: shards(): jnp.einsum('fhqk,fkhd->fhqd', expon.astype(jnp.bfloat16), lax.all_gather(...]
    ppermute x0 -> x18, waiting for transfers between devices: none -> 40 us  [hop(): return lax.ppermute(array, POS, perm)]
    all_to_all x0 -> x3, waiting for transfers between devices: none -> 27.2 us  [the longest x1 14.9 us: shards(): across = lax.all_to_all(packed[8], 'frame', 0, 0, tiled=True)]
    unnamed x6 -> x42, local copies, waits for them, and re-layouts: 29.1 us -> 2.56 us
    pallas_call x0 -> x4, Pallas kernels: none -> 26.2 us  [the longest x1 9.82 us: project(): pl.pallas_call(project_kernel, out_shape=shape(RING, ROWS, SHARE), in_spe...]
    all_to_all x0 -> x3, starting transfers between devices: none -> 21.9 us  [the longest x1 11.8 us: shards(): across = lax.all_to_all(packed[8], 'frame', 0, 0, tiled=True)]
  transfers between devices with their start and end apart: 3 -> 22, of which waited for: 2 -> 11; matrix products, arithmetic and copies ran while one was open for 14% -> 1% of each run, Pallas kernels for 0% -> 9%
where the time goes in v1:
time: 174 us
  waiting for transfers between devices  67.3 us (39%)
  starting transfers between devices  36.7 us (21%)
  Pallas kernels  26.2 us (15%)
  blocking collectives  20 us (11%)
  between operations  13.7 us (8%)
  local copies, waits for them, and re-layouts  7.52 us (4%)
  other arithmetic  2.28 us (1%)
    ppermute x18, waiting for transfers between devices, hop(): return lax.ppermute(array, POS, perm)  40 us
    all_to_all x1, blocking collectives, shards(): whole = lax.all_to_all(out, 'y', 0, 0, tiled=True)  20 us
    all_to_all x1, waiting for transfers between devices, shards(): across = lax.all_to_all(packed[8], 'frame', 0, 0, tiled=True)  14.9 us
    ppermute x18, starting transfers between devices, hop(): return lax.ppermute(array, POS, perm)  14.8 us
    all_to_all x1, starting transfers between devices, shards(): across = lax.all_to_all(packed[8], 'frame', 0, 0, tiled=True)  11.8 us
    pallas_call x1, Pallas kernels, project(): pl.pallas_call(project_kernel, out_shape=shape(RING, ROWS, SHARE), in_spe...  9.82 us
    pallas_call x1, Pallas kernels, spatial(): pl.pallas_call(spatial_kernel, out_shape=[shape(RING, ROWS, 2 * SIZE)] *...  8.34 us
    all_to_all x1, waiting for transfers between devices, weight_share(): rows = lax.all_to_all(sent, POS, 0, 0, tiled=True).reshape(96, SHARE)  6.79 us
  transfers between devices with their start and end apart: 22, of which 11 were waited for; matrix products, arithmetic and copies ran while one was open for 1% of the time, Pallas kernels for 9%

profile of v1, /device:TPU:2, one launch (start us, length us, event | category | flops | bytes accessed | tf_op | source)
XLA Modules:
  0.0 173.7 jit_solution(6333117215063672440)
XLA Ops:
  6.5 0.9 reshape.19
  7.5 0.7 broadcast_in_dim.2
  8.2 4.5 %all-to-all-start = ((bf16[8,12,768]{2,1,0:T(8,128)(2,1)}), bf16[8,12,768]{2,1,0:T(8,128)(2,1)S(1)}, u32[]{:S(2)}, u32[]{:S(2)}) async-start(bf16[8,12,768]{2,1,0:T(8,128)(2,1)} %bitcast.3), calls=%async_computation | async-start | bytes 393216 | tf_op jit(solution)/shard_map/all_to_all | solution.py:205
  12.7 0.0 all-gather.3.cloned.1.call-start
  12.7 6.8 %all-to-all-done = bf16[8,12,768]{2,1,0:T(8,128)(2,1)S(1)} async-done(((bf16[8,12,768]{2,1,0:T(8,128)(2,1)}), bf16[8,12,768]{2,1,0:T(8,128)(2,1)S(1)}, u32[]{:S(2)}, u32[]{:S(2)}) %all-to-all-start) | async-done | bytes 147488 | tf_op jit(solution)/shard_map/all_to_all | solution.py:205
  19.5 0.6 constant_dynamic-slice_fusion
  20.2 0.0 all-gather.3.cloned.1.call-update
  20.2 0.0 copy-done.20
  20.2 1.7 sort.17
  21.9 0.6 pad_add_fusion.place
  22.5 4.6 %pack.1 = (bf16[3,2,192,128]{3,2,1,0:T(8,128)(2,1)}, bf16[3,2,192,128]{3,2,1,0:T(8,128)(2,1)}, bf16[3,2,192,128]{3,2,1,0:T(8,128)(2,1)}, bf16[3,2,192,128]{3,2,1...) custom-call(s32[24]{0:T(128)} %get-tuple-element.17.ids, ...), custom_call_target="tpu_custom_call" | custom-call | bytes 7000000 | tf_op jit(solution)/shard_map/pack/pallas_call | solution.py:56
  27.2 0.0 copy-start.11
  27.2 11.8 %all-to-all-start.1 = ((bf16[32,3,48,128]{3,2,1,0:T(8,128)(2,1)}), bf16[32,3,48,128]{3,2,1,0:T(8,128)(2,1)S(1)}, u32[]{:S(2)}, u32[]{:S(2)}) async-start(bf16[32,3,48,128]{3,2,1,0:T(8,128)(2,1)} %get-tuple-element.28), calls=%async_computation.1 | async-start | bytes 2359296 | tf_op jit(solution)/shard_map/all_to_all | solution.py:222
  38.9 0.6 collective-permute-start
  39.6 2.1 %collective-permute-start.1 = (bf16[3,2,192,128]{3,2,1,0:T(8,128)(2,1)}, bf16[3,2,192,128]{3,2,1,0:T(8,128)(2,1)S(1)}, u32[]{:S(2)}, u32[]{:S(2)}) collective-permute-start(bf16[3,2,192,128]{3,2,1,0:T(8,128)(2,1)} %get-tuple-element.20), channel_id=1, source_target_pairs={{0,4},{1,5},{2,6},{3,7},{4,0},{5,1},{6,2},{7,3},{8,12},{9,13},{10,... | collective-permute-start | bytes 884744 | tf_op jit(solution)/shard_map/ppermute | solution.py:199
  41.6 0.7 collective-permute-start.2
  42.3 0.0 collective-permute-start.3
  42.4 0.0 copy-done.15
  42.4 1.4 collective-permute-start.4
  43.8 12.9 %collective-permute-done.refs_1_ = bf16[3,2,192,128]{3,2,1,0:T(8,128)(2,1)S(1)} collective-permute-done((bf16[3,2,192,128]{3,2,1,0:T(8,128)(2,1)}, bf16[3,2,192,128]{3,2,1,0:T(8,128)(2,1)S(1)}, u32[]{:S(2)}, u32[]{:S(2)}) %collective-permute-start) | collective-permute-done | bytes 294944 | tf_op jit(solution)/shard_map/ppermute | solution.py:199
  56.7 0.0 collective-permute-start.5
  56.7 0.0 collective-permute-done.1.refs_2_
  56.7 0.1 collective-permute-start.6
  56.8 14.9 %all-to-all-done.1.heads = bf16[32,3,48,128]{3,2,1,0:T(8,128)(2,1)S(1)} async-done(((bf16[32,3,48,128]{3,2,1,0:T(8,128)(2,1)}), bf16[32,3,48,128]{3,2,1,0:T(8,128)(2,1)S(1)}, u32[]{:S(2)}, u32[]{:S(2)}) %all-to-all-start.1) | async-done | bytes 1179680 | tf_op jit(solution)/shard_map/all_to_all | solution.py:222
  71.7 1.0 copy-done
  72.7 3.4 %temporal.1 = bf16[32,48,128]{2,1,0:T(8,128)(2,1)} custom-call(bf16[32,3,48,128]{3,2,1,0:T(8,128)(2,1)} %copy-done), custom_call_target="tpu_custom_call" | custom-call | flops 600000000 | bytes 1600000 | tf_op jit(solution)/shard_map/temporal/pallas_call | solution.py:123
  76.1 5.7 %all-to-all-start.2 = ((bf16[32,48,128]{2,1,0:T(8,128)(2,1)}), bf16[32,48,128]{2,1,0:T(8,128)(2,1)S(1)}, u32[]{:S(2)}, u32[]{:S(2)}) async-start(bf16[32,48,128]{2,1,0:T(8,128)(2,1)} %temporal.1), calls=%async_computation.2 | async-start | bytes 786432 | tf_op jit(solution)/shard_map/all_to_all | solution.py:230
  81.8 0.0 collective-permute-done.2.refs_3_
  81.8 0.0 collective-permute-done.3.refs_4_
  81.8 0.0 collective-permute-done.4.refs_5_
  81.9 0.0 collective-permute-done.5.refs_6_
  81.9 0.0 collective-permute-done.6.refs_7_
  81.9 0.6 copy-done.16
  82.5 0.2 copy-done.18
  82.7 8.3 %spatial.1 = (bf16[4,192,256]{2,1,0:T(8,128)(2,1)}, bf16[4,192,256]{2,1,0:T(8,128)(2,1)}) custom-call(s32[2]{0:T(128)} %pad_add_fusion.place, bf16[3,2,192,128]{3,2,1,0:T(8,128)(2,1)} %get-tuple-element.18.refs_0_, bf16[3,2,192,128]{3,2,1,0:T(8,128)(2,1)} %copy-done.12, bf16[3,2,192,128]{3,2,1,0:T(8,128)(2,1)} %copy-done.14, ...), custom_call_target="tpu_custom_call" | custom-call | flops 4800000000 | bytes 4000000 | tf_op jit(solution)/shard_map/spatial/pallas_call | solution.py:97
  91.0 0.0 collective-permute-start.7
  91.0 0.6 collective-permute-start.8
  91.7 1.3 collective-permute-done.7.refs_1_
  93.0 1.3 collective-permute-start.11
  94.3 5.6 %all-to-all-done.2.refs_8_ = bf16[32,48,128]{2,1,0:T(8,128)(2,1)S(1)} async-done(((bf16[32,48,128]{2,1,0:T(8,128)(2,1)}), bf16[32,48,128]{2,1,0:T(8,128)(2,1)S(1)}, u32[]{:S(2)}, u32[]{:S(2)}) %all-to-all-start.2) | async-done | bytes 393248 | tf_op jit(solution)/shard_map/all_to_all | solution.py:230
  99.9 0.9 collective-permute-start.16
  100.7 1.2 collective-permute-start.14
  101.9 2.1 %collective-permute-start.13 = (bf16[4,192,256]{2,1,0:T(8,128)(2,1)}, bf16[4,192,256]{2,1,0:T(8,128)(2,1)S(1)}, u32[]{:S(2)}, u32[]{:S(2)}) collective-permute-start(bf16[4,192,256]{2,1,0:T(8,128)(2,1)} %get-tuple-element.26.refs_0_), channel_id=1, source_target_pairs={{0,6},{1,7},{2,0},{3,1},{4,2},{5,3},{6,4},{7,5},{8,14},{9,15},{10,... | collective-permute-start | bytes 1179656 | tf_op jit(solution)/shard_map/ppermute | solution.py:199
  104.0 0.4 collective-permute-done.8.refs_2_
  104.4 0.0 collective-permute-start.9
  104.4 0.6 collective-permute-done.11.refs_7_
  104.9 0.6 collective-permute-start.10
  105.5 7.8 %collective-permute-done.16.refs_12_ = bf16[32,48,128]{2,1,0:T(8,128)(2,1)S(1)} collective-permute-done((bf16[32,48,128]{2,1,0:T(8,128)(2,1)S(1)}, bf16[32,48,128]{2,1,0:T(8,128)(2,1)S(1)}, u32[]{:S(2)}, u32[]{:S(2)}) %collective-permute-start.16) | collective-permute-done | bytes 393248 | tf_op jit(solution)/shard_map/ppermute | solution.py:199
  113.4 2.5 %collective-permute-start.12 = (bf16[4,192,256]{2,1,0:T(8,128)(2,1)S(1)}, bf16[4,192,256]{2,1,0:T(8,128)(2,1)S(1)}, u32[]{:S(2)}, u32[]{:S(2)}) collective-permute-start(bf16[4,192,256]{2,1,0:T(8,128)(2,1)S(1)} %collective-permute-done.11.refs_7_), channel_id=1, source_target_pairs={{0,6},{1,7},{2,0},{3,1},{4,2},{5,3},{6,4},{7,5},{8,14},{9,15},{10,... | collective-permute-start | bytes 1179656 | tf_op jit(solution)/shard_map/ppermute | solution.py:199
  115.9 0.0 collective-permute-done.14.refs_9_
  115.9 0.1 collective-permute-start.17
  116.0 5.8 %collective-permute-done.13.refs_6_ = bf16[4,192,256]{2,1,0:T(8,128)(2,1)S(1)} collective-permute-done((bf16[4,192,256]{2,1,0:T(8,128)(2,1)}, bf16[4,192,256]{2,1,0:T(8,128)(2,1)S(1)}, u32[]{:S(2)}, u32[]{:S(2)}) %collective-permute-start.13) | collective-permute-done | bytes 393248 | tf_op jit(solution)/shard_map/ppermute | solution.py:199
  121.8 0.6 collective-permute-start.15
  122.4 0.0 collective-permute-done.9.refs_3_
  122.4 8.4 %collective-permute-done.10.refs_4_ = bf16[4,192,256]{2,1,0:T(8,128)(2,1)S(1)} collective-permute-done((bf16[4,192,256]{2,1,0:T(8,128)(2,1)S(1)}, bf16[4,192,256]{2,1,0:T(8,128)(2,1)S(1)}, u32[]{:S(2)}, u32[]{:S(2)}) %collective-permute-start.10) | collective-permute-done | bytes 393248 | tf_op jit(solution)/shard_map/ppermute | solution.py:199
  130.8 0.0 collective-permute-done.12.refs_5_
  130.9 2.8 %collective-permute-done.17.refs_11_ = bf16[16,48,128]{2,1,0:T(8,128)(2,1)S(1)} collective-permute-done((bf16[16,48,128]{2,1,0:T(8,128)(2,1)S(1)}, bf16[16,48,128]{2,1,0:T(8,128)(2,1)S(1)}, u32[]{:S(2)}, u32[]{:S(2)}) %collective-permute-start.17) | collective-permute-done | bytes 196640 | tf_op jit(solution)/shard_map/ppermute | solution.py:199
  133.6 0.7 copy-done.19
  134.3 0.0 collective-permute-done.15.refs_10_
  134.3 0.0 copy-done.4
  134.4 9.8 %project.1 = bf16[4,192,768]{2,1,0:T(8,128)(2,1)} custom-call(s32[24]{0:T(128)} %get-tuple-element.17.ids, s32[2]{0:T(128)} %pad_add_fusion.place, bf16[3072,768]{1,0:T(8,128)(2,1)} %all-gather.3.cloned.1.call-done.weight, bf16[4,192,256]{2,1,0:T(8,128)(2,1)} %get-tuple-element.26.refs_0_, bf16[4,192,256]{2,1,0:T(8,128)(2,1)} %copy-done.4, ...), custom_call_target="tpu_custom_call" | custom-call | flops 3600000000 | bytes 11000000 | tf_op jit(solution)/shard_map/project/pallas_call | solution.py:177
  144.2 20.0 %all_to_all.20 = bf16[4,192,768]{2,1,0:T(8,128)(2,1)S(1)} all-to-all(bf16[4,192,768]{2,1,0:T(8,128)(2,1)} %project.1), channel_id=1, replica_groups=mesh['frame'=32,'y'=4,'core'=2] {'y'}, dimensions={0} | all-to-all | bytes 2359296 | tf_op jit(solution)/shard_map/all_to_all | solution.py:242
  164.2 0.9 copy.6
  165.1 1.7 reshape.24
  (40 shorter events, 0.1 us)
Async XLA Ops:
  6.5 13.7 %copy-start.20 = (s32[24]{0:T(128)S(1)}, s32[24]{0:T(128)}, u32[]{:S(2)}) copy-start(s32[24]{0:T(128)} %param.4) | copy-start | bytes 292
  8.2 11.3 %all-to-all-start = ((bf16[8,12,768]{2,1,0:T(8,128)(2,1)}), bf16[8,12,768]{2,1,0:T(8,128)(2,1)S(1)}, u32[]{:S(2)}, u32[]{:S(2)}) async-start(bf16[8,12,768]{2,1,0:T(8,128)(2,1)} %bitcast.3), calls=%async_computation | async-start | bytes 393216 | tf_op jit(solution)/shard_map/all_to_all | solution.py:205
  12.7 121.7 %all-gather.3.cloned.1.call-start = ((), (), s32[]{:S(2)}) async-start(), calls=%async_computation.4 | async-start | bytes 4792320 | tf_op jit(solution)/shard_map/all_gather | solution.py:207
  27.1 15.2 %copy-start.17 = (bf16[3,2,192,128]{3,2,1,0:T(8,128)(2,1)S(1)}, bf16[3,2,192,128]{3,2,1,0:T(8,128)(2,1)}, u32[]{:S(2)}) copy-start(bf16[3,2,192,128]{3,2,1,0:T(8,128)(2,1)} %get-tuple-element.22) | copy-start | bytes 884740
  27.1 15.2 %copy-start.15 = (bf16[3,2,192,128]{3,2,1,0:T(8,128)(2,1)S(1)}, bf16[3,2,192,128]{3,2,1,0:T(8,128)(2,1)}, u32[]{:S(2)}) copy-start(bf16[3,2,192,128]{3,2,1,0:T(8,128)(2,1)} %get-tuple-element.23) | copy-start | bytes 884740
  27.2 29.5 %copy-start.13 = (bf16[3,2,192,128]{3,2,1,0:T(8,128)(2,1)S(1)}, bf16[3,2,192,128]{3,2,1,0:T(8,128)(2,1)}, u32[]{:S(2)}) copy-start(bf16[3,2,192,128]{3,2,1,0:T(8,128)(2,1)} %get-tuple-element.24) | copy-start | bytes 884740
  27.2 29.6 %copy-start.11 = (bf16[3,2,192,128]{3,2,1,0:T(8,128)(2,1)S(1)}, bf16[3,2,192,128]{3,2,1,0:T(8,128)(2,1)}, u32[]{:S(2)}) copy-start(bf16[3,2,192,128]{3,2,1,0:T(8,128)(2,1)} %get-tuple-element.25) | copy-start | bytes 884740
  27.2 44.5 %all-to-all-start.1 = ((bf16[32,3,48,128]{3,2,1,0:T(8,128)(2,1)}), bf16[32,3,48,128]{3,2,1,0:T(8,128)(2,1)S(1)}, u32[]{:S(2)}, u32[]{:S(2)}) async-start(bf16[32,3,48,128]{3,2,1,0:T(8,128)(2,1)} %get-tuple-element.28), calls=%async_computation.1 | async-start | bytes 2359296 | tf_op jit(solution)/shard_map/all_to_all | solution.py:222
  38.9 17.8 %collective-permute-start = (bf16[3,2,192,128]{3,2,1,0:T(8,128)(2,1)}, bf16[3,2,192,128]{3,2,1,0:T(8,128)(2,1)S(1)}, u32[]{:S(2)}, u32[]{:S(2)}) collective-permute-start(bf16[3,2,192,128]{3,2,1,0:T(8,128)(2,1)} %get-tuple-element.19), channel_id=1, source_target_pairs={{0,2},{1,3},{2,4},{3,5},{4,6},{5,7},{6,0},{7,1},{8,10},{9,11},{10,... | collective-permute-start | bytes 884744 | tf_op jit(solution)/shard_map/ppermute | solution.py:199
  39.6 17.1 %collective-permute-start.1 = (bf16[3,2,192,128]{3,2,1,0:T(8,128)(2,1)}, bf16[3,2,192,128]{3,2,1,0:T(8,128)(2,1)S(1)}, u32[]{:S(2)}, u32[]{:S(2)}) collective-permute-start(bf16[3,2,192,128]{3,2,1,0:T(8,128)(2,1)} %get-tuple-element.20), channel_id=1, source_target_pairs={{0,4},{1,5},{2,6},{3,7},{4,0},{5,1},{6,2},{7,3},{8,12},{9,13},{10,... | collective-permute-start | bytes 884744 | tf_op jit(solution)/shard_map/ppermute | solution.py:199
  41.6 40.2 %collective-permute-start.2 = (bf16[3,2,192,128]{3,2,1,0:T(8,128)(2,1)}, bf16[3,2,192,128]{3,2,1,0:T(8,128)(2,1)S(1)}, u32[]{:S(2)}, u32[]{:S(2)}) collective-permute-start(bf16[3,2,192,128]{3,2,1,0:T(8,128)(2,1)} %get-tuple-element.21), channel_id=1, source_target_pairs={{0,6},{1,7},{2,0},{3,1},{4,2},{5,3},{6,4},{7,5},{8,14},{9,15},{10,... | collective-permute-start | bytes 884744 | tf_op jit(solution)/shard_map/ppermute | solution.py:199
  42.3 39.5 %collective-permute-start.3 = (bf16[3,2,192,128]{3,2,1,0:T(8,128)(2,1)S(1)}, bf16[3,2,192,128]{3,2,1,0:T(8,128)(2,1)S(1)}, u32[]{:S(2)}, u32[]{:S(2)}) collective-permute-start(bf16[3,2,192,128]{3,2,1,0:T(8,128)(2,1)S(1)} %copy-done.17), channel_id=1, source_target_pairs={{0,1},{1,0},{2,3},{3,2},{4,5},{5,4},{6,7},{7,6},{8,9},{9,8},{10,11... | collective-permute-start | bytes 884744 | tf_op jit(solution)/shard_map/ppermute | solution.py:199
  42.4 39.5 %collective-permute-start.4 = (bf16[3,2,192,128]{3,2,1,0:T(8,128)(2,1)S(1)}, bf16[3,2,192,128]{3,2,1,0:T(8,128)(2,1)}, u32[]{:S(2)}, u32[]{:S(2)}) collective-permute-start(bf16[3,2,192,128]{3,2,1,0:T(8,128)(2,1)S(1)} %copy-done.15), channel_id=1, source_target_pairs={{0,3},{1,2},{2,5},{3,4},{4,7},{5,6},{6,1},{7,0},{8,11},{9,10},{10,... | collective-permute-start | bytes 884744 | tf_op jit(solution)/shard_map/ppermute | solution.py:199
  56.7 25.2 %copy-start.12 = (bf16[3,2,192,128]{3,2,1,0:T(8,128)(2,1)}, bf16[3,2,192,128]{3,2,1,0:T(8,128)(2,1)S(1)}, u32[]{:S(2)}) copy-start(bf16[3,2,192,128]{3,2,1,0:T(8,128)(2,1)S(1)} %collective-permute-done.refs_1_) | copy-start | bytes 884740
  56.7 25.2 %collective-permute-start.5 = (bf16[3,2,192,128]{3,2,1,0:T(8,128)(2,1)S(1)}, bf16[3,2,192,128]{3,2,1,0:T(8,128)(2,1)}, u32[]{:S(2)}, u32[]{:S(2)}) collective-permute-start(bf16[3,2,192,128]{3,2,1,0:T(8,128)(2,1)S(1)} %copy-done.13), channel_id=1, source_target_pairs={{0,5},{1,4},{2,7},{3,6},{4,1},{5,0},{6,3},{7,2},{8,13},{9,12},{10,... | collective-permute-start | bytes 884744 | tf_op jit(solution)/shard_map/ppermute | solution.py:199
  56.7 25.2 %copy-start.14 = (bf16[3,2,192,128]{3,2,1,0:T(8,128)(2,1)}, bf16[3,2,192,128]{3,2,1,0:T(8,128)(2,1)S(1)}, u32[]{:S(2)}) copy-start(bf16[3,2,192,128]{3,2,1,0:T(8,128)(2,1)S(1)} %collective-permute-done.1.refs_2_) | copy-start | bytes 884740
  56.7 25.1 %collective-permute-start.6 = (bf16[3,2,192,128]{3,2,1,0:T(8,128)(2,1)S(1)}, bf16[3,2,192,128]{3,2,1,0:T(8,128)(2,1)}, u32[]{:S(2)}, u32[]{:S(2)}) collective-permute-start(bf16[3,2,192,128]{3,2,1,0:T(8,128)(2,1)S(1)} %copy-done.11), channel_id=1, source_target_pairs={{0,7},{1,6},{2,1},{3,0},{4,3},{5,2},{6,5},{7,4},{8,15},{9,14},{10,... | collective-permute-start | bytes 884744 | tf_op jit(solution)/shard_map/ppermute | solution.py:199
  71.7 1.0 copy-start
  76.1 23.7 %all-to-all-start.2 = ((bf16[32,48,128]{2,1,0:T(8,128)(2,1)}), bf16[32,48,128]{2,1,0:T(8,128)(2,1)S(1)}, u32[]{:S(2)}, u32[]{:S(2)}) async-start(bf16[32,48,128]{2,1,0:T(8,128)(2,1)} %temporal.1), calls=%async_computation.2 | async-start | bytes 786432 | tf_op jit(solution)/shard_map/all_to_all | solution.py:230
  81.8 0.7 copy-start.16
  81.8 0.9 copy-start.18
  91.0 1.9 %collective-permute-start.7 = (bf16[4,192,256]{2,1,0:T(8,128)(2,1)}, bf16[4,192,256]{2,1,0:T(8,128)(2,1)S(1)}, u32[]{:S(2)}, u32[]{:S(2)}) collective-permute-start(bf16[4,192,256]{2,1,0:T(8,128)(2,1)} %get-tuple-element.27), channel_id=1, source_target_pairs={{0,1},{1,0},{2,3},{3,2},{4,5},{5,4},{6,7},{7,6},{8,9},{9,8},{10,11... | collective-permute-start | bytes 1179656 | tf_op jit(solution)/shard_map/ppermute | solution.py:199
  91.0 13.3 %collective-permute-start.8 = (bf16[4,192,256]{2,1,0:T(8,128)(2,1)}, bf16[4,192,256]{2,1,0:T(8,128)(2,1)S(1)}, u32[]{:S(2)}, u32[]{:S(2)}) collective-permute-start(bf16[4,192,256]{2,1,0:T(8,128)(2,1)} %get-tuple-element.26.refs_0_), channel_id=1, source_target_pairs={{0,2},{1,3},{2,4},{3,5},{4,6},{5,7},{6,0},{7,1},{8,10},{9,11},{10,... | collective-permute-start | bytes 1179656 | tf_op jit(solution)/shard_map/ppermute | solution.py:199
  93.0 41.3 %copy-start.4 = (bf16[4,192,256]{2,1,0:T(8,128)(2,1)}, bf16[4,192,256]{2,1,0:T(8,128)(2,1)S(1)}, u32[]{:S(2)}) copy-start(bf16[4,192,256]{2,1,0:T(8,128)(2,1)S(1)} %collective-permute-done.7.refs_1_) | copy-start | bytes 1179652
  93.0 12.0 %collective-permute-start.11 = (bf16[4,192,256]{2,1,0:T(8,128)(2,1)S(1)}, bf16[4,192,256]{2,1,0:T(8,128)(2,1)S(1)}, u32[]{:S(2)}, u32[]{:S(2)}) collective-permute-start(bf16[4,192,256]{2,1,0:T(8,128)(2,1)S(1)} %collective-permute-done.7.refs_1_), channel_id=1, source_target_pairs={{0,6},{1,7},{2,0},{3,1},{4,2},{5,3},{6,4},{7,5},{8,14},{9,15},{10,... | collective-permute-start | bytes 1179656 | tf_op jit(solution)/shard_map/ppermute | solution.py:199
  99.9 34.5 %copy-start.1 = (bf16[32,48,128]{2,1,0:T(8,128)(2,1)}, bf16[32,48,128]{2,1,0:T(8,128)(2,1)S(1)}, u32[]{:S(2)}) copy-start(bf16[32,48,128]{2,1,0:T(8,128)(2,1)S(1)} %all-to-all-done.2.refs_8_) | copy-start | bytes 1179652
  99.9 13.5 %collective-permute-start.16 = (bf16[32,48,128]{2,1,0:T(8,128)(2,1)S(1)}, bf16[32,48,128]{2,1,0:T(8,128)(2,1)S(1)}, u32[]{:S(2)}, u32[]{:S(2)}) collective-permute-start(bf16[32,48,128]{2,1,0:T(8,128)(2,1)S(1)} %all-to-all-done.2.refs_8_), channel_id=1, source_target_pairs={{0,6},{1,7},{2,0},{3,1},{4,2},{5,3},{6,4},{7,5},{8,14},{9,15},{10,... | collective-permute-start | bytes 1179656 | tf_op jit(solution)/shard_map/ppermute | solution.py:199
  100.7 15.2 %collective-permute-start.14 = (bf16[32,48,128]{2,1,0:T(8,128)(2,1)S(1)}, bf16[32,48,128]{2,1,0:T(8,128)(2,1)S(1)}, u32[]{:S(2)}, u32[]{:S(2)}) collective-permute-start(bf16[32,48,128]{2,1,0:T(8,128)(2,1)S(1)} %all-to-all-done.2.refs_8_), channel_id=1, source_target_pairs={{0,2},{1,3},{2,4},{3,5},{4,6},{5,7},{6,0},{7,1},{8,10},{9,11},{10,... | collective-permute-start | bytes 1179656 | tf_op jit(solution)/shard_map/ppermute | solution.py:199
  101.9 19.9 %collective-permute-start.13 = (bf16[4,192,256]{2,1,0:T(8,128)(2,1)}, bf16[4,192,256]{2,1,0:T(8,128)(2,1)S(1)}, u32[]{:S(2)}, u32[]{:S(2)}) collective-permute-start(bf16[4,192,256]{2,1,0:T(8,128)(2,1)} %get-tuple-element.26.refs_0_), channel_id=1, source_target_pairs={{0,6},{1,7},{2,0},{3,1},{4,2},{5,3},{6,4},{7,5},{8,14},{9,15},{10,... | collective-permute-start | bytes 1179656 | tf_op jit(solution)/shard_map/ppermute | solution.py:199
  104.4 30.0 %copy-start.5 = (bf16[4,192,256]{2,1,0:T(8,128)(2,1)}, bf16[4,192,256]{2,1,0:T(8,128)(2,1)S(1)}, u32[]{:S(2)}) copy-start(bf16[4,192,256]{2,1,0:T(8,128)(2,1)S(1)} %collective-permute-done.8.refs_2_) | copy-start | bytes 1179652
  104.4 18.0 %collective-permute-start.9 = (bf16[4,192,256]{2,1,0:T(8,128)(2,1)S(1)}, bf16[4,192,256]{2,1,0:T(8,128)(2,1)S(1)}, u32[]{:S(2)}, u32[]{:S(2)}) collective-permute-start(bf16[4,192,256]{2,1,0:T(8,128)(2,1)S(1)} %collective-permute-done.7.refs_1_), channel_id=1, source_target_pairs={{0,2},{1,3},{2,4},{3,5},{4,6},{5,7},{6,0},{7,1},{8,10},{9,11},{10,... | collective-permute-start | bytes 1179656 | tf_op jit(solution)/shard_map/ppermute | solution.py:199
  104.9 29.4 %copy-start.6 = (bf16[4,192,256]{2,1,0:T(8,128)(2,1)}, bf16[4,192,256]{2,1,0:T(8,128)(2,1)S(1)}, u32[]{:S(2)}) copy-start(bf16[4,192,256]{2,1,0:T(8,128)(2,1)S(1)} %collective-permute-done.11.refs_7_) | copy-start | bytes 1179652
  104.9 25.9 %collective-permute-start.10 = (bf16[4,192,256]{2,1,0:T(8,128)(2,1)S(1)}, bf16[4,192,256]{2,1,0:T(8,128)(2,1)S(1)}, u32[]{:S(2)}, u32[]{:S(2)}) collective-permute-start(bf16[4,192,256]{2,1,0:T(8,128)(2,1)S(1)} %collective-permute-done.8.refs_2_), channel_id=1, source_target_pairs={{0,2},{1,3},{2,4},{3,5},{4,6},{5,7},{6,0},{7,1},{8,10},{9,11},{10,... | collective-permute-start | bytes 1179656 | tf_op jit(solution)/shard_map/ppermute | solution.py:199
  113.4 21.0 %copy-start.2 = (bf16[32,48,128]{2,1,0:T(8,128)(2,1)}, bf16[32,48,128]{2,1,0:T(8,128)(2,1)S(1)}, u32[]{:S(2)}) copy-start(bf16[32,48,128]{2,1,0:T(8,128)(2,1)S(1)} %collective-permute-done.16.refs_12_) | copy-start | bytes 1179652
  113.4 17.5 %collective-permute-start.12 = (bf16[4,192,256]{2,1,0:T(8,128)(2,1)S(1)}, bf16[4,192,256]{2,1,0:T(8,128)(2,1)S(1)}, u32[]{:S(2)}, u32[]{:S(2)}) collective-permute-start(bf16[4,192,256]{2,1,0:T(8,128)(2,1)S(1)} %collective-permute-done.11.refs_7_), channel_id=1, source_target_pairs={{0,6},{1,7},{2,0},{3,1},{4,2},{5,3},{6,4},{7,5},{8,14},{9,15},{10,... | collective-permute-start | bytes 1179656 | tf_op jit(solution)/shard_map/ppermute | solution.py:199
  115.9 18.5 %copy-start.3 = (bf16[32,48,128]{2,1,0:T(8,128)(2,1)}, bf16[32,48,128]{2,1,0:T(8,128)(2,1)S(1)}, u32[]{:S(2)}) copy-start(bf16[32,48,128]{2,1,0:T(8,128)(2,1)S(1)} %collective-permute-done.14.refs_9_) | copy-start | bytes 1179652
  115.9 17.7 %collective-permute-start.17 = (bf16[16,48,128]{2,1,0:T(8,128)(2,1)S(1)}, bf16[16,48,128]{2,1,0:T(8,128)(2,1)S(1)}, u32[]{:S(2)}, u32[]{:S(2)}) collective-permute-start(bf16[16,48,128]{2,1,0:T(8,128)(2,1)S(1)} %slice.9), channel_id=1, source_target_pairs={{0,6},{1,7},{2,0},{3,1},{4,2},{5,3},{6,4},{7,5},{8,14},{9,15},{10,... | collective-permute-start | bytes 589832 | tf_op jit(solution)/shard_map/ppermute | solution.py:199
  121.8 12.6 %copy-start.7 = (bf16[4,192,256]{2,1,0:T(8,128)(2,1)}, bf16[4,192,256]{2,1,0:T(8,128)(2,1)S(1)}, u32[]{:S(2)}) copy-start(bf16[4,192,256]{2,1,0:T(8,128)(2,1)S(1)} %collective-permute-done.13.refs_6_) | copy-start | bytes 1179652
  121.8 12.5 %collective-permute-start.15 = (bf16[16,48,128]{2,1,0:T(8,128)(2,1)S(1)}, bf16[16,48,128]{2,1,0:T(8,128)(2,1)}, u32[]{:S(2)}, u32[]{:S(2)}) collective-permute-start(bf16[16,48,128]{2,1,0:T(8,128)(2,1)S(1)} %slice.8), channel_id=1, source_target_pairs={{0,2},{1,3},{2,4},{3,5},{4,6},{5,7},{6,0},{7,1},{8,10},{9,11},{10,... | collective-permute-start | bytes 589832 | tf_op jit(solution)/shard_map/ppermute | solution.py:199
  122.4 12.0 %copy-start.8 = (bf16[4,192,256]{2,1,0:T(8,128)(2,1)}, bf16[4,192,256]{2,1,0:T(8,128)(2,1)S(1)}, u32[]{:S(2)}) copy-start(bf16[4,192,256]{2,1,0:T(8,128)(2,1)S(1)} %collective-permute-done.9.refs_3_) | copy-start | bytes 1179652
  130.8 3.5 %copy-start.9 = (bf16[4,192,256]{2,1,0:T(8,128)(2,1)}, bf16[4,192,256]{2,1,0:T(8,128)(2,1)S(1)}, u32[]{:S(2)}) copy-start(bf16[4,192,256]{2,1,0:T(8,128)(2,1)S(1)} %collective-permute-done.10.refs_4_) | copy-start | bytes 1179652
  130.9 2.8 %copy-start.10 = (bf16[4,192,256]{2,1,0:T(8,128)(2,1)}, bf16[4,192,256]{2,1,0:T(8,128)(2,1)S(1)}, u32[]{:S(2)}) copy-start(bf16[4,192,256]{2,1,0:T(8,128)(2,1)S(1)} %collective-permute-done.12.refs_5_) | copy-start | bytes 1179652
  133.6 0.7 copy-start.19
Sparse Core Ops, SparseCore 0:
  20.3 86.7 all-gather.2

commit v2 on v1

v2 whole, which is shorter than its diff:
```python
import jax
import jax.numpy as jnp
from jax import lax
from jax.experimental import pallas as pl
from jax.experimental.pallas import tpu as pltpu
from jax.sharding import Mesh, PartitionSpec as P

HEADS = 24
SIZE = 128
SPATIAL = 16
D = 3072
FRAMES = 32
ROWS = 192
RING = 4
SHARE = D // RING
GROUP = 48
EXP_SCALE = 1.4426950408889634 * SIZE ** -0.5
POS = ("y", "core")
BF16 = jnp.bfloat16
F32 = jnp.float32
VMEM = pl.BlockSpec(memory_space=pltpu.VMEM)
SMEM = pl.BlockSpec(memory_space=pltpu.SMEM)
ANY = pl.BlockSpec(memory_space=pl.ANY)


def shape(*dims, dtype=BF16):
    return jax.ShapeDtypeStruct(dims, dtype)


def params():
    return pltpu.CompilerParams(vmem_limit_bytes=56 * 1024 * 1024)


def cost(flops, nbytes, exps=0):
    return pl.CostEstimate(flops=flops, bytes_accessed=nbytes, transcendentals=exps)


def rank_heads(kinds, ids):
    spatial_next, temporal_next = jnp.int32(0), jnp.int32(SPATIAL)
    for head in range(HEADS):
        kind = kinds[head]
        ids[jnp.where(kind == 0, spatial_next, temporal_next)] = head
        spatial_next, temporal_next = spatial_next + 1 - kind, temporal_next + kind


def head_columns(ids, rank):
    return pl.ds(pl.multiple_of(ids[rank] * SIZE, SIZE), SIZE)


def run_copies(pairs, sems):
    copies = [pltpu.make_async_copy(a, b, sems.at[i]) for i, (a, b) in enumerate(pairs)]
    for copy in copies:
        copy.start()
    return copies


def pack_temporal_kernel(kinds, qkv, out, ids, sems):
    rank_heads(kinds, ids)
    pairs = []
    for head in range(HEADS - SPATIAL):
        columns = head_columns(ids, SPATIAL + head)
        for piece in range(RING):
            rows = pl.ds(piece * GROUP, GROUP)
            pairs.append((qkv.at[:, rows, columns], out.at[head * RING + piece]))
    for copy in run_copies(pairs, sems):
        copy.wait()


def pack_temporal(kinds, qkv):
    return pl.pallas_call(
        pack_temporal_kernel,
        out_shape=shape(FRAMES, 3, GROUP, SIZE),
        in_specs=[SMEM, ANY],
        out_specs=ANY,
        scratch_shapes=[pltpu.SMEM((HEADS,), jnp.int32), pltpu.SemaphoreType.DMA((FRAMES,))],
        compiler_params=params(),
        cost_estimate=cost(0, 2_400_000),
        name="pack_temporal",
    )(kinds, qkv)


def pack_spatial_kernel(kinds, qkv, *refs):
    outs, (ids, sems) = refs[:8], refs[8:]
    rank_heads(kinds, ids)
    y, core = lax.axis_index("y"), lax.axis_index("core")
    pairs = []
    for part in range(2):
        for step in range(RING):
            to = lax.rem(y + step, RING) * 2 + lax.rem(core + part, 2)
            for head in range(2):
                columns = head_columns(ids, to * 2 + head)
                pairs.append((qkv.at[:, :, columns], outs[part * RING + step].at[:, head]))
    for copy in run_copies(pairs, sems):
        copy.wait()


def pack_spatial(kinds, qkv):
    return pl.pallas_call(
        pack_spatial_kernel,
        out_shape=[shape(3, 2, ROWS, SIZE)] * 8,
        in_specs=[SMEM, ANY],
        out_specs=[ANY] * 8,
        scratch_shapes=[pltpu.SMEM((HEADS,), jnp.int32), pltpu.SemaphoreType.DMA((16,))],
        compiler_params=params(),
        cost_estimate=cost(0, 4_800_000),
        name="pack_spatial",
    )(kinds, qkv)


def attend(query, key, value_ones, keep=None):
    score = lax.dot_general(query, key, (((1,), (1,)), ((), ())), preferred_element_type=F32)
    if keep is not None:
        score = jnp.where(keep, score, -1e30)
    top = jnp.max(score, axis=1, keepdims=True)
    weight = jnp.exp2((score - top) * EXP_SCALE).astype(BF16)
    both = jnp.dot(weight, value_ones, preferred_element_type=F32)
    return (both[:, :SIZE] / both[:, SIZE:]).astype(BF16)


def spatial_kernel(*refs):
    chunks, outs = refs[:8], refs[8:]
    y = lax.axis_index("y")
    ones = jnp.ones((8 * ROWS, SIZE), BF16)
    for head in range(2):
        key = jnp.concatenate([chunk[1, head] for chunk in chunks], axis=0)
        value = jnp.concatenate([chunk[2, head] for chunk in chunks], axis=0)
        value_ones = jnp.concatenate([value, ones], axis=1)
        for pair in range(4):
            two = (pair * 2, pair * 2 + 1)
            query = jnp.concatenate([chunks[i][0, head] for i in two], axis=0)
            result = attend(query, key, value_ones)
            for n, i in enumerate(two):
                origin = lax.rem(y + RING - i % RING, RING)
                outs[i // RING][origin, :, head * SIZE : (head + 1) * SIZE] = result[
                    n * ROWS : (n + 1) * ROWS
                ]


def spatial(chunks):
    return pl.pallas_call(
        spatial_kernel,
        out_shape=[shape(RING, ROWS, 2 * SIZE)] * 2,
        in_specs=[VMEM] * 8,
        out_specs=[VMEM] * 2,
        compiler_params=params(),
        cost_estimate=cost(4_800_000_000, 4_000_000, 4_700_000),
        name="spatial",
    )(*chunks)


def temporal_kernel(heads, out):
    span = 16
    count = FRAMES * span
    same = lax.broadcasted_iota(jnp.int32, (count, count), 0) % span == (
        lax.broadcasted_iota(jnp.int32, (count, count), 1) % span
    )
    ones = jnp.ones((count, SIZE), BF16)
    for piece in range(GROUP // span):
        rows = slice(piece * span, (piece + 1) * span)
        query, key, value = (heads[:, c, rows].reshape(count, SIZE) for c in range(3))
        result = attend(query, key, jnp.concatenate([value, ones], axis=1), same)
        out[:, rows] = result.reshape(FRAMES, span, SIZE)


def temporal(heads):
    return pl.pallas_call(
        temporal_kernel,
        out_shape=shape(FRAMES, GROUP, SIZE),
        in_specs=[VMEM],
        out_specs=VMEM,
        compiler_params=params(),
        cost_estimate=cost(600_000_000, 1_600_000, 800_000),
        name="temporal",
    )(heads)


def arrange_kernel(own, behind, ahead, far_low, far_high, out, sems):
    z, x = lax.axis_index("z"), lax.axis_index("x")
    pairs = []
    for step, halves in enumerate(
        ((own.at[:4], own.at[4:]), (behind.at[:4], behind.at[4:]), (far_low, far_high), (ahead.at[:4], ahead.at[4:]))
    ):
        x_from = lax.rem(x + RING - step, RING)
        for slab in range(8):
            z_from = lax.rem(z + 8 - slab, 8)
            pairs.append((halves[slab // 4].at[slab % 4], out.at[z_from * 4 + x_from]))
    for copy in run_copies(pairs, sems):
        copy.wait()


def arrange(*blocks):
    return pl.pallas_call(
        arrange_kernel,
        out_shape=shape(FRAMES, 96, SHARE // 2),
        in_specs=[ANY] * 5,
        out_specs=ANY,
        scratch_shapes=[pltpu.SemaphoreType.DMA((FRAMES,))],
        compiler_params=params(),
        cost_estimate=cost(0, 4_800_000),
        name="arrange",
    )(*blocks)


def weight_pairs(ids, ranks, halves, target):
    core = lax.axis_index("core")
    pairs = []
    for slot, rank in enumerate(ranks):
        rows = head_columns(ids, rank)
        for part, half in enumerate(halves):
            start = pl.multiple_of(lax.rem(core + part, 2) * (SHARE // 2), SIZE)
            to = target.at[pl.ds(slot * SIZE, SIZE), pl.ds(start, SHARE // 2)]
            pairs.append((half.at[rows], to))
    return pairs


def project_spatial_kernel(kinds, weight_own, weight_other, *refs):
    blocks = refs[:8]
    total, weight_temporal, ids, held, tokens, sems = refs[8:]
    y, core = lax.axis_index("y"), lax.axis_index("core")
    rank_heads(kinds, ids)
    ranks = []
    for step in range(RING):
        origin = lax.rem(y + RING - step, RING)
        for part in range(2):
            first = origin * 4 + lax.rem(core + part, 2) * 2
            ranks += [first, first + 1]
    halves = (weight_own, weight_other)
    pairs = weight_pairs(ids, ranks, halves, held)
    pairs += weight_pairs(ids, range(SPATIAL, HEADS), halves, weight_temporal)
    copies = run_copies(pairs, sems)
    for slot, block in enumerate(blocks):
        tokens[:, :, slot * 256 : (slot + 1) * 256] = block[...]
    for copy in copies:
        copy.wait()
    left = tokens[...].reshape(RING * ROWS, SPATIAL * SIZE)
    for n in range(SHARE // 256):
        columns = slice(n * 256, (n + 1) * 256)
        product = jnp.dot(left, held[:, columns], preferred_element_type=F32)
        total[:, :, columns] = product.reshape(RING, ROWS, 256)


def project_spatial(kinds, weight_own, weight_other, blocks):
    return pl.pallas_call(
        project_spatial_kernel,
        out_shape=[shape(RING, ROWS, SHARE, dtype=F32), shape(D - SPATIAL * SIZE, SHARE)],
        in_specs=[SMEM, ANY, ANY] + [VMEM] * 8,
        out_specs=[VMEM, ANY],
        scratch_shapes=[
            pltpu.SMEM((HEADS,), jnp.int32),
            pltpu.VMEM((SPATIAL * SIZE, SHARE), BF16),
            pltpu.VMEM((RING, ROWS, SPATIAL * SIZE), BF16),
            pltpu.SemaphoreType.DMA((2 * HEADS,)),
        ],
        compiler_params=params(),
        cost_estimate=cost(2_400_000_000, 11_000_000),
        name="project_spatial",
    )(kinds, weight_own, weight_other, *blocks)


def project_temporal(total, weight, halves, steps, pieces):
    count = len(steps)

    def kernel(total, weight, *refs):
        ins, outs, held, sems = refs[: 2 * count], refs[2 * count : -2], refs[-2], refs[-1]
        y = lax.axis_index("y")
        pairs = [
            (total.at[lax.rem(y + RING - step, RING)], held.at[i]) for i, step in enumerate(steps)
        ]
        copies = run_copies(pairs, sems)
        lefts = []
        for i in range(count):
            heads = []
            for half in ins[2 * i : 2 * i + 2]:
                heads += [half[h * 4 : h * 4 + 4].reshape(ROWS, SIZE) for h in range(4)]
            lefts.append(jnp.concatenate(heads, axis=1))
        left = jnp.concatenate(lefts, axis=0)
        for copy in copies:
            copy.wait()
        rows = ROWS // pieces
        for n in range(SHARE // 256):
            columns = slice(n * 256, (n + 1) * 256)
            product = jnp.dot(left, weight[:, columns], preferred_element_type=F32)
            for i in range(count):
                whole = held[i, :, columns] + product[i * ROWS : (i + 1) * ROWS]
                for piece in range(pieces):
                    outs[i * pieces + piece][:, columns] = whole[
                        piece * rows : (piece + 1) * rows
                    ].astype(BF16)

    return pl.pallas_call(
        kernel,
        out_shape=[shape(ROWS // pieces, SHARE)] * (count * pieces),
        in_specs=[ANY] + [VMEM] * (2 * count + 1),
        out_specs=[VMEM] * (count * pieces),
        scratch_shapes=[
            pltpu.VMEM((count, ROWS, SHARE), F32),
            pltpu.SemaphoreType.DMA((count,)),
        ],
        compiler_params=params(),
        cost_estimate=cost(300_000_000 * count, 2_000_000 + 1_300_000 * count),
        name="project_temporal",
    )(total, weight, *[half for pair in halves for half in pair])


def finish_kernel(own, behind, ahead, far_low, far_high, out, sems):
    y = lax.axis_index("y")
    half = ROWS // 2

    def columns(step):
        return pl.ds(pl.multiple_of(lax.rem(y + RING - step, RING) * SHARE, SIZE), SHARE)

    pairs = [
        (own, out.at[:, columns(0)]),
        (behind, out.at[:, columns(1)]),
        (far_low, out.at[:half, columns(2)]),
        (far_high, out.at[half:, columns(2)]),
        (ahead, out.at[:, columns(3)]),
    ]
    for copy in run_copies(pairs, sems):
        copy.wait()


def finish(*blocks):
    return pl.pallas_call(
        finish_kernel,
        out_shape=shape(ROWS, D),
        in_specs=[ANY] * 5,
        out_specs=ANY,
        scratch_shapes=[pltpu.SemaphoreType.DMA((5,))],
        compiler_params=params(),
        cost_estimate=cost(0, 2_400_000),
        name="finish",
    )(*blocks)


def hop(array, axis, steps):
    size = lax.axis_size(axis)
    return lax.ppermute(array, axis, [(i, (i + steps) % size) for i in range(size)])


def hop_over(array, steps):
    perm = [
        (y * 2 + core, ((y + steps) % RING) * 2 + 1 - core)
        for y in range(RING)
        for core in range(2)
    ]
    return lax.ppermute(array, POS, perm)


def weight_halves(out_weight):
    sent = jnp.transpose(out_weight.reshape(12, 8, SHARE // 2), (1, 0, 2))
    slab = lax.all_to_all(sent, POS, 0, 0, tiled=True).reshape(96, SHARE // 2)
    forward, backward = [slab], []
    for _ in range(4):
        forward.append(hop(forward[-1], "z", 1))
    for _ in range(3):
        backward.append(hop(backward[-1] if backward else slab, "z", -1))
    slabs = jnp.stack(forward + backward[::-1])
    behind, ahead = hop(slabs, "x", 1), hop(slabs, "x", -1)
    far_low, far_high = hop(behind[:4], "x", 1), hop(ahead[4:], "x", -1)
    own = arrange(slabs, behind, ahead, far_low, far_high).reshape(D, SHARE // 2)
    return own, hop(own, "core", 1)


def shards(qkv, head_kind, out_weight):
    qkv = qkv.reshape(3, ROWS, D)
    across = lax.all_to_all(pack_temporal(head_kind, qkv), ("z", "x"), 0, 0, tiled=True)

    packed = pack_spatial(head_kind, qkv)
    far_same = hop(packed[2], "y", 1)
    far_cross = hop(packed[6], "y", -1)
    chunks = [
        packed[0],
        hop(packed[1], "y", 1),
        hop(far_same, "y", 1),
        hop(packed[3], "y", -1),
        hop(packed[4], "core", 1),
        hop_over(packed[5], 1),
        hop_over(far_cross, -1),
        hop_over(packed[7], -1),
    ]
    weight_own, weight_other = weight_halves(out_weight)

    mine, other = spatial(chunks)
    theirs = hop(other, "core", 1)
    mine_behind, mine_ahead = hop(mine, "y", 1), hop(mine, "y", -1)
    theirs_behind, theirs_ahead = hop(theirs, "y", 1), hop(theirs, "y", -1)
    mine_far = hop(mine_behind, "y", 1)
    theirs_far = hop(theirs_ahead, "y", -1)

    back = lax.all_to_all(temporal(across), ("z", "x"), 0, 0, tiled=True)
    low, high = back[:16], back[16:]
    low_behind, high_ahead = hop(low, "y", 1), hop(high, "y", -1)
    high_behind, low_ahead = hop(high, "y", 1), hop(low, "y", -1)
    low_far, high_far = hop(low_behind, "y", 1), hop(high_ahead, "y", -1)

    blocks = [mine, theirs, mine_behind, theirs_behind, mine_far, theirs_far, mine_ahead, theirs_ahead]
    total, weight_temporal = project_spatial(head_kind, weight_own, weight_other, blocks)
    out_far = project_temporal(total, weight_temporal, [(low_far, high_far)], [2], 2)
    out_behind, out_ahead = project_temporal(
        total,
        weight_temporal,
        [(low_behind, high_behind), (low_ahead, high_ahead)],
        [1, 3],
        1,
    )
    (out_own,) = project_temporal(total, weight_temporal, [(low, high)], [0], 1)
    from_far_low = hop(hop(out_far[0], "y", 1), "y", 1)
    from_far_high = hop(hop(out_far[1], "y", -1), "y", -1)
    from_behind, from_ahead = hop(out_ahead, "y", 1), hop(out_behind, "y", -1)
    whole = finish(out_own, from_behind, from_ahead, from_far_low, from_far_high)
    return whole.reshape(1, ROWS, D)


def solution(mesh):
    split = Mesh(mesh.devices.reshape(8, 4, 4, 2), ("z", "x", "y", "core"))
    placed = (P(None, ("z", "x"), POS, None), P(), P(("z", "x", "y", "core"), None))
    return jax.shard_map(
        shards, mesh=split, in_specs=placed, out_specs=P(("z", "x"), POS, None), check_vma=False
    )
```

time: 174 us -> 489 us (2.81); the launches traced: 174 us -> 480 us
  Pallas kernels: 26.2 us -> 300 us
  starting transfers between devices: 36.7 us -> 77.1 us
  waiting for transfers between devices: 67.3 us -> 91.8 us
  blocking collectives: 20 us -> 0 us
  between operations: 13.7 us -> 0.99 us
    pallas_call x2 -> x8, Pallas kernels: 14.5 us -> 288 us  [the longest x1 73.5 us: pack_spatial(): pl.pallas_call(pack_spatial_kernel, out_shape=[shape(3, 2, ROWS, SIZE)] *...]
    ppermute x18 -> x40, waiting for transfers between devices: 40 us -> 91.8 us  [the longest x37 86.9 us: hop(): lax.ppermute(array, axis, [(i, (i + steps) % size) for i in range(size)])]
    ppermute x18 -> x40, starting transfers between devices: 14.8 us -> 51.8 us  [the longest x37 50.5 us: hop(): lax.ppermute(array, axis, [(i, (i + steps) % size) for i in range(size)])]
    all_to_all x3, waiting for transfers between devices: 27.2 us -> 0.01 us  [the longest x1 0.01 us: weight_halves(): slab = lax.all_to_all(sent, POS, 0, 0, tiled=True).reshape(96, SHARE // 2)]
    all_to_all x1 -> x0, blocking collectives: 20 us -> none  [shards(): whole = lax.all_to_all(out, 'y', 0, 0, tiled=True)]
    unnamed x42 -> x76, local copies, waits for them, and re-layouts: 2.56 us -> 9.25 us
  transfers between devices with their start and end apart: 22 -> 43, of which waited for: 11 -> 18; matrix products, arithmetic and copies ran while one was open for 1% -> 0% of each run, Pallas kernels for 9% -> 55%
where the time goes in v2:
time: 489 us; the launch traced here: 480 us
  Pallas kernels  300 us (61%)
  waiting for transfers between devices  91.8 us (19%)
  starting transfers between devices  77.1 us (16%)
  local copies, waits for them, and re-layouts  10.1 us (2%)
    ppermute x37, waiting for transfers between devices, hop(): lax.ppermute(array, axis, [(i, (i + steps) % size) for i in range(size)])  86.9 us
    pallas_call x1, Pallas kernels, pack_spatial(): pl.pallas_call(pack_spatial_kernel, out_shape=[shape(3, 2, ROWS, SIZE)] *...  73.5 us
    pallas_call x1, Pallas kernels, arrange(): pl.pallas_call(arrange_kernel, out_shape=shape(FRAMES, 96, SHARE // 2), i...  72.9 us
    pallas_call x1, Pallas kernels, project_spatial(): pl.pallas_call(project_spatial_kernel, out_shape=[shape(RING, ROWS, SHARE...  55.2 us
    ppermute x37, starting transfers between devices, hop(): lax.ppermute(array, axis, [(i, (i + steps) % size) for i in range(size)])  50.5 us
    pallas_call x1, Pallas kernels, pack_temporal(): pl.pallas_call(pack_temporal_kernel, out_shape=shape(FRAMES, 3, GROUP, SI...  37.9 us
    pallas_call x1, Pallas kernels, finish(): pl.pallas_call(finish_kernel, out_shape=shape(ROWS, D), in_specs=[ANY] *...  36.9 us
    pallas_call x3, Pallas kernels, project_temporal(): pl.pallas_call(kernel, out_shape=[shape(ROWS // pieces, SHARE)] * (count...  12.1 us
  transfers between devices with their start and end apart: 43, of which 18 were waited for; matrix products, arithmetic and copies ran while one was open for 0% of the time, Pallas kernels for 55%

profile of v2, /device:TPU:2, one launch (start us, length us, event | category | flops | bytes accessed | tf_op | source)
XLA Modules:
  0.0 480.0 jit_solution(3565468256687696426)
XLA Ops:
  0.0 0.9 copy.6
  0.9 0.7 copy.8
  1.6 4.5 all-to-all-start
  6.0 37.9 %pack_temporal.1 = bf16[32,3,48,128]{3,2,1,0:T(8,128)(2,1)} custom-call(s32[24]{0:T(128)} %kinds.5, bf16[3,192,3072]{2,1,0:T(8,128)(2,1)} %bitcast.23), custom_call_target="tpu_custom_call" | custom-call | bytes 2400000 | tf_op jit(solution)/shard_map/pack_temporal/pallas_call | solution.py:70
  43.9 11.6 %all-to-all-start.1 = ((bf16[32,3,48,128]{3,2,1,0:T(8,128)(2,1)}), bf16[32,3,48,128]{3,2,1,0:T(8,128)(2,1)S(1)}, u32[]{:S(2)}, u32[]{:S(2)}) async-start(bf16[32,3,48,128]{3,2,1,0:T(8,128)(2,1)} %pack_temporal.1), calls=%async_computation.1 | async-start | bytes 2359296 | tf_op jit(solution)/shard_map/all_to_all | solution.py:367
  55.6 1.5 collective-permute-start
  57.1 1.8 collective-permute-start.4
  58.9 26.4 %collective-permute-done = bf16[96,384]{1,0:T(8,128)(2,1)S(1)} collective-permute-done((bf16[96,384]{1,0:T(8,128)(2,1)S(1)}, bf16[96,384]{1,0:T(8,128)(2,1)S(1)}, u32[]{:S(2)}, u32[]{:S(2)}) %collective-permute-start) | collective-permute-done | bytes 73760 | tf_op jit(solution)/shard_map/ppermute | solution.py:338
  85.4 3.3 collective-permute-start.5
  88.7 2.2 collective-permute-done.1
  90.9 3.3 collective-permute-start.6
  94.3 2.2 collective-permute-done.2
  96.5 5.5 %collective-permute-done.3 = bf16[96,384]{1,0:T(8,128)(2,1)S(1)} collective-permute-done((bf16[96,384]{1,0:T(8,128)(2,1)S(1)}, bf16[96,384]{1,0:T(8,128)(2,1)S(1)}, u32[]{:S(2)}, u32[]{:S(2)}) %collective-permute-start.3) | collective-permute-done | bytes 73760 | tf_op jit(solution)/shard_map/ppermute | solution.py:338
  102.1 1.0 collective-permute-start.8
  103.1 1.1 collective-permute-start.7
  104.2 11.4 %collective-permute-done.8.ahead = bf16[8,96,384]{2,1,0:T(8,128)(2,1)S(1)} collective-permute-done((bf16[8,96,384]{2,1,0:T(8,128)(2,1)S(1)}, bf16[8,96,384]{2,1,0:T(8,128)(2,1)S(1)}, u32[]{:S(2)}, u32[]{:S(2)}) %collective-permute-start.8) | collective-permute-done | bytes 589856 | tf_op jit(solution)/shard_map/ppermute | solution.py:338
  116.1 1.8 collective-permute-start.9
  117.9 73.5 %pack_spatial.1 = (bf16[3,2,192,128]{3,2,1,0:T(8,128)(2,1)}, bf16[3,2,192,128]{3,2,1,0:T(8,128)(2,1)}, bf16[3,2,192,128]{3,2,1,0:T(8,128)(2,1)}, bf16[3,2,192,12...) custom-call(s32[24]{0:T(128)} %kinds.5, ...), custom_call_target="tpu_custom_call" | custom-call | bytes 4800000 | tf_op jit(solution)/shard_map/pack_spatial/pallas_call | solution.py:98
  191.4 1.7 collective-permute-start.13
  193.1 0.7 copy-done.8
  193.9 0.7 copy-done.9
  194.6 72.9 %arrange.1 = bf16[32,96,384]{2,1,0:T(8,128)(2,1)} custom-call(bf16[8,96,384]{2,1,0:T(8,128)(2,1)} %copy-done.5, bf16[8,96,384]{2,1,0:T(8,128)(2,1)} %copy-done.1, bf16[8,96,384]{2,1,0:T(8,128)(2,1)} %copy-done, bf16[4,96,384]{2,1,0:T(8,128)(2,1)} %copy-done.9, bf16[4,96,384]{2,1,0:T(8,128)(2,1)} %copy-done.8), custom_call_target="tpu_custom_call" | custom-call | bytes 4800000 | tf_op jit(solution)/shard_map/arrange/pallas_call | solution.py:192
  267.6 1.9 collective-permute-start.18
  269.9 2.8 collective-permute-start.15
  272.7 4.9 %collective-permute-done.18 = bf16[3,2,192,128]{3,2,1,0:T(8,128)(2,1)S(1)} collective-permute-done((bf16[3,2,192,128]{3,2,1,0:T(8,128)(2,1)S(1)}, bf16[3,2,192,128]{3,2,1,0:T(8,128)(2,1)S(1)}, u32[]{:S(2)}, u32[]{:S(2)}) %collective-permute-start.18) | collective-permute-done | bytes 294944 | tf_op jit(solution)/shard_map/ppermute | solution.py:338
  277.8 1.9 collective-permute-done.12.refs_1_
  279.7 1.0 collective-permute-start.20
  280.7 3.3 collective-permute-done.15.refs_3_
  284.0 1.5 collective-permute-start.14
  285.6 2.4 collective-permute-done.17.refs_5_
  288.0 1.4 collective-permute-done.20.refs_7_
  289.5 5.1 %collective-permute-done.14.refs_2_ = bf16[3,2,192,128]{3,2,1,0:T(8,128)(2,1)S(1)} collective-permute-done((bf16[3,2,192,128]{3,2,1,0:T(8,128)(2,1)S(1)}, bf16[3,2,192,128]{3,2,1,0:T(8,128)(2,1)S(1)}, u32[]{:S(2)}, u32[]{:S(2)}) %collective-permute-start.14) | collective-permute-done | bytes 294944 | tf_op jit(solution)/shard_map/ppermute | solution.py:338
  294.5 1.0 collective-permute-done.19.refs_6_
  295.6 0.7 copy-done.33
  296.2 8.3 %spatial.1 = (bf16[4,192,256]{2,1,0:T(8,128)(2,1)}, bf16[4,192,256]{2,1,0:T(8,128)(2,1)}) custom-call(bf16[3,2,192,128]{3,2,1,0:T(8,128)(2,1)} %get-tuple-element.21.refs_0_, bf16[3,2,192,128]{3,2,1,0:T(8,128)(2,1)} %copy-done.24, bf16[3,2,192,128]{3,2,1,0:T(8,128)(2,1)} %copy-done.32, bf16[3,2,192,128]{3,2,1,0:T(8,128)(2,1)} %copy-done.26, ...), custom_call_target="tpu_custom_call" | custom-call | flops 4800000000 | bytes 4000000 | tf_op jit(solution)/shard_map/spatial/pallas_call | solution.py:140
  305.1 1.0 copy-done.2
  306.1 3.4 temporal.1
  309.5 9.3 %all-to-all-start.2 = ((bf16[32,48,128]{2,1,0:T(8,128)(2,1)}), bf16[32,48,128]{2,1,0:T(8,128)(2,1)S(1)}, u32[]{:S(2)}, u32[]{:S(2)}) async-start(bf16[32,48,128]{2,1,0:T(8,128)(2,1)} %temporal.1), calls=%async_computation.2 | async-start | bytes 786432 | tf_op jit(solution)/shard_map/all_to_all | solution.py:391
  318.8 1.5 collective-permute-start.22
  320.3 1.8 collective-permute-start.25
  322.1 1.6 collective-permute-start.27
  323.7 7.2 %collective-permute-done.22.refs_2_ = bf16[4,192,256]{2,1,0:T(8,128)(2,1)S(1)} collective-permute-done((bf16[4,192,256]{2,1,0:T(8,128)(2,1)}, bf16[4,192,256]{2,1,0:T(8,128)(2,1)S(1)}, u32[]{:S(2)}, u32[]{:S(2)}) %collective-permute-start.22) | collective-permute-done | bytes 393248 | tf_op jit(solution)/shard_map/ppermute | solution.py:338
  331.2 1.2 collective-permute-start.23
  332.6 3.0 collective-permute-start.26
  335.7 5.5 %collective-permute-done.27.refs_6_ = bf16[4,192,256]{2,1,0:T(8,128)(2,1)} collective-permute-done((bf16[4,192,256]{2,1,0:T(8,128)(2,1)}, bf16[4,192,256]{2,1,0:T(8,128)(2,1)}, u32[]{:S(2)}, u32[]{:S(2)}) %collective-permute-start.27) | collective-permute-done | bytes 393248 | tf_op jit(solution)/shard_map/ppermute | solution.py:338
  341.1 1.2 collective-permute-start.28
  342.3 2.0 collective-permute-done.24.refs_4_
  344.6 8.1 %collective-permute-done.23.refs_3_ = bf16[4,192,256]{2,1,0:T(8,128)(2,1)} collective-permute-done((bf16[4,192,256]{2,1,0:T(8,128)(2,1)}, bf16[4,192,256]{2,1,0:T(8,128)(2,1)}, u32[]{:S(2)}, u32[]{:S(2)}) %collective-permute-start.23) | collective-permute-done | bytes 393248 | tf_op jit(solution)/shard_map/ppermute | solution.py:338
  352.7 3.2 collective-permute-start.30
  355.9 0.9 collective-permute-done.28.refs_0_
  356.8 3.5 collective-permute-start.35
  360.3 1.4 copy-done.18
  361.7 55.2 %project_spatial.1 = (f32[4,192,768]{2,1,0:T(8,128)}, bf16[1024,768]{1,0:T(8,128)(2,1)}) custom-call(s32[24]{0:T(128)} %kinds.5, bf16[3072,384]{1,0:T(8,128)(2,1)} %bitcast.26, bf16[3072,384]{1,0:T(8,128)(2,1)} %copy-done.18, bf16[4,192,256]{2,1,0:T(8,128)(2,1)} %get-tuple-element.29.refs_0_, bf16[4,192,256]{2,1,0:T(8,128)(2,1)} %collective-permute-done.21.refs_1_, ...), custom_call_target="tpu_custom_call" | custom-call | flops 2400000000 | bytes 11000000 | tf_op jit(solution)/shard_map/project_spatial/pallas_call | solution.py:243
  417.0 0.6 copy-done.14
  417.7 3.8 project_temporal.5
  421.6 3.2 collective-permute-start.38
  424.9 0.7 copy-done.12
  425.5 0.7 copy-done.13
  426.2 4.5 project_temporal.4
  430.8 3.2 collective-permute-start.33
  434.0 3.2 collective-permute-start.39
  437.2 3.8 project_temporal.3.own
  441.9 0.7 copy-done.7
  442.6 36.9 %finish.1 = bf16[192,3072]{1,0:T(8,128)(2,1)} custom-call(bf16[192,768]{1,0:T(8,128)(2,1)} %project_temporal.3.own, bf16[192,768]{1,0:T(8,128)(2,1)} %copy-done.6, bf16[192,768]{1,0:T(8,128)(2,1)} %copy-done.7, bf16[96,768]{1,0:T(8,128)(2,1)} %copy-done.16, bf16[96,768]{1,0:T(8,128)(2,1)} %copy-done.17), custom_call_target="tpu_custom_call" | custom-call | bytes 2400000 | tf_op jit(solution)/shard_map/finish/pallas_call | solution.py:324
  (116 shorter events, 4.0 us)
Async XLA Ops:
  1.6 42.3 %all-to-all-start = ((bf16[8,12,384]{2,1,0:T(8,128)(2,1)}), bf16[8,12,384]{2,1,0:T(8,128)(2,1)S(1)}, u32[]{:S(2)}, u32[]{:S(2)}) async-start(bf16[8,12,384]{2,1,0:T(8,128)(2,1)} %bitcast.22), calls=%async_computation | async-start | bytes 196608 | tf_op jit(solution)/shard_map/all_to_all | solution.py:352
  43.9 261.2 %all-to-all-start.1 = ((bf16[32,3,48,128]{3,2,1,0:T(8,128)(2,1)}), bf16[32,3,48,128]{3,2,1,0:T(8,128)(2,1)S(1)}, u32[]{:S(2)}, u32[]{:S(2)}) async-start(bf16[32,3,48,128]{3,2,1,0:T(8,128)(2,1)} %pack_temporal.1), calls=%async_computation.1 | async-start | bytes 2359296 | tf_op jit(solution)/shard_map/all_to_all | solution.py:367
  55.6 29.8 %collective-permute-start = (bf16[96,384]{1,0:T(8,128)(2,1)S(1)}, bf16[96,384]{1,0:T(8,128)(2,1)S(1)}, u32[]{:S(2)}, u32[]{:S(2)}) collective-permute-start(bf16[96,384]{1,0:T(8,128)(2,1)S(1)} %reshape.16), channel_id=1, source_target_pairs={{0,32},{32,64},{64,96},{96,128},{128,160},{160,192},{192,224},{224... | collective-permute-start | bytes 221192 | tf_op jit(solution)/shard_map/ppermute | solution.py:338
  57.1 28.3 %collective-permute-start.4 = (bf16[96,384]{1,0:T(8,128)(2,1)S(1)}, bf16[96,384]{1,0:T(8,128)(2,1)S(1)}, u32[]{:S(2)}, u32[]{:S(2)}) collective-permute-start(bf16[96,384]{1,0:T(8,128)(2,1)S(1)} %reshape.16), channel_id=1, source_target_pairs={{0,224},{32,0},{64,32},{96,64},{128,96},{160,128},{192,160},{224,1... | collective-permute-start | bytes 221192 | tf_op jit(solution)/shard_map/ppermute | solution.py:338
  85.3 5.6 %collective-permute-start.1 = (bf16[96,384]{1,0:T(8,128)(2,1)S(1)}, bf16[96,384]{1,0:T(8,128)(2,1)S(1)}, u32[]{:S(2)}, u32[]{:S(2)}) collective-permute-start(bf16[96,384]{1,0:T(8,128)(2,1)S(1)} %collective-permute-done), channel_id=1, source_target_pairs={{0,32},{32,64},{64,96},{96,128},{128,160},{160,192},{192,224},{224... | collective-permute-start | bytes 221192 | tf_op jit(solution)/shard_map/ppermute | solution.py:338
  85.4 5.6 %collective-permute-start.5 = (bf16[96,384]{1,0:T(8,128)(2,1)S(1)}, bf16[96,384]{1,0:T(8,128)(2,1)S(1)}, u32[]{:S(2)}, u32[]{:S(2)}) collective-permute-start(bf16[96,384]{1,0:T(8,128)(2,1)S(1)} %collective-permute-done.4), channel_id=1, source_target_pairs={{0,224},{32,0},{64,32},{96,64},{128,96},{160,128},{192,160},{224,1... | collective-permute-start | bytes 221192 | tf_op jit(solution)/shard_map/ppermute | solution.py:338
  90.9 5.6 %collective-permute-start.2 = (bf16[96,384]{1,0:T(8,128)(2,1)S(1)}, bf16[96,384]{1,0:T(8,128)(2,1)S(1)}, u32[]{:S(2)}, u32[]{:S(2)}) collective-permute-start(bf16[96,384]{1,0:T(8,128)(2,1)S(1)} %collective-permute-done.1), channel_id=1, source_target_pairs={{0,32},{32,64},{64,96},{96,128},{128,160},{160,192},{192,224},{224... | collective-permute-start | bytes 221192 | tf_op jit(solution)/shard_map/ppermute | solution.py:338
  90.9 11.1 %collective-permute-start.6 = (bf16[96,384]{1,0:T(8,128)(2,1)S(1)}, bf16[96,384]{1,0:T(8,128)(2,1)S(1)}, u32[]{:S(2)}, u32[]{:S(2)}) collective-permute-start(bf16[96,384]{1,0:T(8,128)(2,1)S(1)} %collective-permute-done.5), channel_id=1, source_target_pairs={{0,224},{32,0},{64,32},{96,64},{128,96},{160,128},{192,160},{224,1... | collective-permute-start | bytes 221192 | tf_op jit(solution)/shard_map/ppermute | solution.py:338
  96.5 5.6 %collective-permute-start.3 = (bf16[96,384]{1,0:T(8,128)(2,1)S(1)}, bf16[96,384]{1,0:T(8,128)(2,1)S(1)}, u32[]{:S(2)}, u32[]{:S(2)}) collective-permute-start(bf16[96,384]{1,0:T(8,128)(2,1)S(1)} %collective-permute-done.2), channel_id=1, source_target_pairs={{0,32},{32,64},{64,96},{96,128},{128,160},{160,192},{192,224},{224... | collective-permute-start | bytes 221192 | tf_op jit(solution)/shard_map/ppermute | solution.py:338
  102.1 89.2 %copy-start.5 = (bf16[8,96,384]{2,1,0:T(8,128)(2,1)}, bf16[8,96,384]{2,1,0:T(8,128)(2,1)S(1)}, u32[]{:S(2)}) copy-start(bf16[8,96,384]{2,1,0:T(8,128)(2,1)S(1)} %bitcast_dynamic-update-slice_fusion.own) | copy-start | bytes 1769476
  102.1 13.5 %collective-permute-start.8 = (bf16[8,96,384]{2,1,0:T(8,128)(2,1)S(1)}, bf16[8,96,384]{2,1,0:T(8,128)(2,1)S(1)}, u32[]{:S(2)}, u32[]{:S(2)}) collective-permute-start(bf16[8,96,384]{2,1,0:T(8,128)(2,1)S(1)} %bitcast_dynamic-update-slice_fusion.own), channel_id=1, source_target_pairs={{0,24},{8,0},{16,8},{24,16},{1,25},{9,1},{17,9},{25,17},{2,26},{10... | collective-permute-start | bytes 1769480 | tf_op jit(solution)/shard_map/ppermute | solution.py:338
  103.1 12.9 %collective-permute-start.7 = (bf16[8,96,384]{2,1,0:T(8,128)(2,1)S(1)}, bf16[8,96,384]{2,1,0:T(8,128)(2,1)S(1)}, u32[]{:S(2)}, u32[]{:S(2)}) collective-permute-start(bf16[8,96,384]{2,1,0:T(8,128)(2,1)S(1)} %bitcast_dynamic-update-slice_fusion.own), channel_id=1, source_target_pairs={{0,8},{8,16},{16,24},{24,0},{1,9},{9,17},{17,25},{25,1},{2,10},{10... | collective-permute-start | bytes 1769480 | tf_op jit(solution)/shard_map/ppermute | solution.py:338
  115.6 75.7 %copy-start = (bf16[8,96,384]{2,1,0:T(8,128)(2,1)}, bf16[8,96,384]{2,1,0:T(8,128)(2,1)S(1)}, u32[]{:S(2)}) copy-start(bf16[8,96,384]{2,1,0:T(8,128)(2,1)S(1)} %collective-permute-done.8.ahead) | copy-start | bytes 1769476
  115.6 77.5 %collective-permute-start.10 = (bf16[4,96,384]{2,1,0:T(8,128)(2,1)S(1)}, bf16[4,96,384]{2,1,0:T(8,128)(2,1)S(1)}, u32[]{:S(2)}, u32[]{:S(2)}) collective-permute-start(bf16[4,96,384]{2,1,0:T(8,128)(2,1)S(1)} %slice.17), channel_id=1, source_target_pairs={{0,24},{8,0},{16,8},{24,16},{1,25},{9,1},{17,9},{25,17},{2,26},{10... | collective-permute-start | bytes 884744 | tf_op jit(solution)/shard_map/ppermute | solution.py:338
  116.0 77.1 %copy-start.1 = (bf16[8,96,384]{2,1,0:T(8,128)(2,1)}, bf16[8,96,384]{2,1,0:T(8,128)(2,1)S(1)}, u32[]{:S(2)}) copy-start(bf16[8,96,384]{2,1,0:T(8,128)(2,1)S(1)} %collective-permute-done.7.behind) | copy-start | bytes 1769476
  116.1 77.1 %collective-permute-start.9 = (bf16[4,96,384]{2,1,0:T(8,128)(2,1)S(1)}, bf16[4,96,384]{2,1,0:T(8,128)(2,1)S(1)}, u32[]{:S(2)}, u32[]{:S(2)}) collective-permute-start(bf16[4,96,384]{2,1,0:T(8,128)(2,1)S(1)} %slice.16), channel_id=1, source_target_pairs={{0,8},{8,16},{16,24},{24,0},{1,9},{9,17},{17,25},{25,1},{2,10},{10... | collective-permute-start | bytes 884744 | tf_op jit(solution)/shard_map/ppermute | solution.py:338
  191.4 76.2 %copy-start.29 = (bf16[3,2,192,128]{3,2,1,0:T(8,128)(2,1)S(1)}, bf16[3,2,192,128]{3,2,1,0:T(8,128)(2,1)}, u32[]{:S(2)}) copy-start(bf16[3,2,192,128]{3,2,1,0:T(8,128)(2,1)} %get-tuple-element.27) | copy-start | bytes 884740
  191.4 78.1 %copy-start.27 = (bf16[3,2,192,128]{3,2,1,0:T(8,128)(2,1)S(1)}, bf16[3,2,192,128]{3,2,1,0:T(8,128)(2,1)}, u32[]{:S(2)}) copy-start(bf16[3,2,192,128]{3,2,1,0:T(8,128)(2,1)} %get-tuple-element.22) | copy-start | bytes 884740
  191.4 78.5 %copy-start.25 = (bf16[3,2,192,128]{3,2,1,0:T(8,128)(2,1)S(1)}, bf16[3,2,192,128]{3,2,1,0:T(8,128)(2,1)}, u32[]{:S(2)}) copy-start(bf16[3,2,192,128]{3,2,1,0:T(8,128)(2,1)} %get-tuple-element.24) | copy-start | bytes 884740
  191.4 81.3 %copy-start.23 = (bf16[3,2,192,128]{3,2,1,0:T(8,128)(2,1)S(1)}, bf16[3,2,192,128]{3,2,1,0:T(8,128)(2,1)}, u32[]{:S(2)}) copy-start(bf16[3,2,192,128]{3,2,1,0:T(8,128)(2,1)} %get-tuple-element.25) | copy-start | bytes 884740
  191.4 86.3 %copy-start.22 = (bf16[3,2,192,128]{3,2,1,0:T(8,128)(2,1)S(1)}, bf16[3,2,192,128]{3,2,1,0:T(8,128)(2,1)}, u32[]{:S(2)}) copy-start(bf16[3,2,192,128]{3,2,1,0:T(8,128)(2,1)} %get-tuple-element.26) | copy-start | bytes 884740
  191.4 88.3 %copy-start.21 = (bf16[3,2,192,128]{3,2,1,0:T(8,128)(2,1)S(1)}, bf16[3,2,192,128]{3,2,1,0:T(8,128)(2,1)}, u32[]{:S(2)}) copy-start(bf16[3,2,192,128]{3,2,1,0:T(8,128)(2,1)} %get-tuple-element.28) | copy-start | bytes 884740
  191.4 81.3 %collective-permute-start.13 = (bf16[3,2,192,128]{3,2,1,0:T(8,128)(2,1)}, bf16[3,2,192,128]{3,2,1,0:T(8,128)(2,1)S(1)}, u32[]{:S(2)}, u32[]{:S(2)}) collective-permute-start(bf16[3,2,192,128]{3,2,1,0:T(8,128)(2,1)} %get-tuple-element.23), channel_id=1, source_target_pairs={{0,2},{2,4},{4,6},{6,0},{1,3},{3,5},{5,7},{7,1},{8,10},{10,12},{12... | collective-permute-start | bytes 884744 | tf_op jit(solution)/shard_map/ppermute | solution.py:338
  267.5 92.8 %collective-permute-start.11 = (bf16[3072,384]{1,0:T(8,128)(2,1)}, bf16[3072,384]{1,0:T(8,128)(2,1)S(1)}, u32[]{:S(2)}, u32[]{:S(2)}) collective-permute-start(bf16[3072,384]{1,0:T(8,128)(2,1)} %bitcast.25), channel_id=1, source_target_pairs={{0,1},{1,0},{2,3},{3,2},{4,5},{5,4},{6,7},{7,6},{8,9},{9,8},{10,11... | collective-permute-start | bytes 7077896 | tf_op jit(solution)/shard_map/ppermute | solution.py:338
  267.6 10.1 %collective-permute-start.18 = (bf16[3,2,192,128]{3,2,1,0:T(8,128)(2,1)S(1)}, bf16[3,2,192,128]{3,2,1,0:T(8,128)(2,1)S(1)}, u32[]{:S(2)}, u32[]{:S(2)}) collective-permute-start(bf16[3,2,192,128]{3,2,1,0:T(8,128)(2,1)S(1)} %copy-done.29), channel_id=1, source_target_pairs={{0,6},{2,0},{4,2},{6,4},{1,7},{3,1},{5,3},{7,5},{8,14},{10,8},{12,... | collective-permute-start | bytes 884744 | tf_op jit(solution)/shard_map/ppermute | solution.py:338
  269.5 10.2 %collective-permute-start.12 = (bf16[3,2,192,128]{3,2,1,0:T(8,128)(2,1)S(1)}, bf16[3,2,192,128]{3,2,1,0:T(8,128)(2,1)S(1)}, u32[]{:S(2)}, u32[]{:S(2)}) collective-permute-start(bf16[3,2,192,128]{3,2,1,0:T(8,128)(2,1)S(1)} %copy-done.27), channel_id=1, source_target_pairs={{0,2},{2,4},{4,6},{6,0},{1,3},{3,5},{5,7},{7,1},{8,10},{10,12},{12... | collective-permute-start | bytes 884744 | tf_op jit(solution)/shard_map/ppermute | solution.py:338
  269.9 14.1 %collective-permute-start.15 = (bf16[3,2,192,128]{3,2,1,0:T(8,128)(2,1)S(1)}, bf16[3,2,192,128]{3,2,1,0:T(8,128)(2,1)S(1)}, u32[]{:S(2)}, u32[]{:S(2)}) collective-permute-start(bf16[3,2,192,128]{3,2,1,0:T(8,128)(2,1)S(1)} %copy-done.25), channel_id=1, source_target_pairs={{0,6},{2,0},{4,2},{6,4},{1,7},{3,1},{5,3},{7,5},{8,14},{10,8},{12,... | collective-permute-start | bytes 884744 | tf_op jit(solution)/shard_map/ppermute | solution.py:338
  272.7 12.7 %collective-permute-start.16 = (bf16[3,2,192,128]{3,2,1,0:T(8,128)(2,1)S(1)}, bf16[3,2,192,128]{3,2,1,0:T(8,128)(2,1)S(1)}, u32[]{:S(2)}, u32[]{:S(2)}) collective-permute-start(bf16[3,2,192,128]{3,2,1,0:T(8,128)(2,1)S(1)} %copy-done.23), channel_id=1, source_target_pairs={{0,1},{1,0},{2,3},{3,2},{4,5},{5,4},{6,7},{7,6},{8,9},{9,8},{10,11... | collective-permute-start | bytes 884744 | tf_op jit(solution)/shard_map/ppermute | solution.py:338
  277.7 10.3 %collective-permute-start.17 = (bf16[3,2,192,128]{3,2,1,0:T(8,128)(2,1)S(1)}, bf16[3,2,192,128]{3,2,1,0:T(8,128)(2,1)S(1)}, u32[]{:S(2)}, u32[]{:S(2)}) collective-permute-start(bf16[3,2,192,128]{3,2,1,0:T(8,128)(2,1)S(1)} %copy-done.22), channel_id=1, source_target_pairs={{0,3},{1,2},{2,5},{3,4},{4,7},{5,6},{6,1},{7,0},{8,11},{9,10},{10,... | collective-permute-start | bytes 884744 | tf_op jit(solution)/shard_map/ppermute | solution.py:347
  279.7 15.9 %copy-start.24 = (bf16[3,2,192,128]{3,2,1,0:T(8,128)(2,1)}, bf16[3,2,192,128]{3,2,1,0:T(8,128)(2,1)S(1)}, u32[]{:S(2)}) copy-start(bf16[3,2,192,128]{3,2,1,0:T(8,128)(2,1)S(1)} %collective-permute-done.12.refs_1_) | copy-start | bytes 884740
  279.7 9.8 %collective-permute-start.20 = (bf16[3,2,192,128]{3,2,1,0:T(8,128)(2,1)S(1)}, bf16[3,2,192,128]{3,2,1,0:T(8,128)(2,1)S(1)}, u32[]{:S(2)}, u32[]{:S(2)}) collective-permute-start(bf16[3,2,192,128]{3,2,1,0:T(8,128)(2,1)S(1)} %copy-done.21), channel_id=1, source_target_pairs={{0,7},{1,6},{2,1},{3,0},{4,3},{5,2},{6,5},{7,4},{8,15},{9,14},{10,... | collective-permute-start | bytes 884744 | tf_op jit(solution)/shard_map/ppermute | solution.py:347
  284.0 11.5 %copy-start.26 = (bf16[3,2,192,128]{3,2,1,0:T(8,128)(2,1)}, bf16[3,2,192,128]{3,2,1,0:T(8,128)(2,1)S(1)}, u32[]{:S(2)}) copy-start(bf16[3,2,192,128]{3,2,1,0:T(8,128)(2,1)S(1)} %collective-permute-done.15.refs_3_) | copy-start | bytes 884740
  284.0 10.5 %collective-permute-start.14 = (bf16[3,2,192,128]{3,2,1,0:T(8,128)(2,1)S(1)}, bf16[3,2,192,128]{3,2,1,0:T(8,128)(2,1)S(1)}, u32[]{:S(2)}, u32[]{:S(2)}) collective-permute-start(bf16[3,2,192,128]{3,2,1,0:T(8,128)(2,1)S(1)} %collective-permute-done.13), channel_id=1, source_target_pairs={{0,2},{2,4},{4,6},{6,0},{1,3},{3,5},{5,7},{7,1},{8,10},{10,12},{12... | collective-permute-start | bytes 884744 | tf_op jit(solution)/shard_map/ppermute | solution.py:338
  285.5 10.1 %copy-start.28 = (bf16[3,2,192,128]{3,2,1,0:T(8,128)(2,1)}, bf16[3,2,192,128]{3,2,1,0:T(8,128)(2,1)S(1)}, u32[]{:S(2)}) copy-start(bf16[3,2,192,128]{3,2,1,0:T(8,128)(2,1)S(1)} %collective-permute-done.16.refs_4_) | copy-start | bytes 884740
  285.5 10.1 %collective-permute-start.19 = (bf16[3,2,192,128]{3,2,1,0:T(8,128)(2,1)S(1)}, bf16[3,2,192,128]{3,2,1,0:T(8,128)(2,1)S(1)}, u32[]{:S(2)}, u32[]{:S(2)}) collective-permute-start(bf16[3,2,192,128]{3,2,1,0:T(8,128)(2,1)S(1)} %collective-permute-done.18), channel_id=1, source_target_pairs={{0,7},{1,6},{2,1},{3,0},{4,3},{5,2},{6,5},{7,4},{8,15},{9,14},{10,... | collective-permute-start | bytes 884744 | tf_op jit(solution)/shard_map/ppermute | solution.py:347
  288.0 7.5 %copy-start.30 = (bf16[3,2,192,128]{3,2,1,0:T(8,128)(2,1)}, bf16[3,2,192,128]{3,2,1,0:T(8,128)(2,1)S(1)}, u32[]{:S(2)}) copy-start(bf16[3,2,192,128]{3,2,1,0:T(8,128)(2,1)S(1)} %collective-permute-done.17.refs_5_) | copy-start | bytes 884740
  289.5 6.1 %copy-start.31 = (bf16[3,2,192,128]{3,2,1,0:T(8,128)(2,1)}, bf16[3,2,192,128]{3,2,1,0:T(8,128)(2,1)S(1)}, u32[]{:S(2)}) copy-start(bf16[3,2,192,128]{3,2,1,0:T(8,128)(2,1)S(1)} %collective-permute-done.20.refs_7_) | copy-start | bytes 884740
  304.6 15.8 %collective-permute-start.21 = (bf16[4,192,256]{2,1,0:T(8,128)(2,1)}, bf16[4,192,256]{2,1,0:T(8,128)(2,1)}, u32[]{:S(2)}, u32[]{:S(2)}) collective-permute-start(bf16[4,192,256]{2,1,0:T(8,128)(2,1)} %get-tuple-element.30), channel_id=1, source_target_pairs={{0,1},{1,0},{2,3},{3,2},{4,5},{5,4},{6,7},{7,6},{8,9},{9,8},{10,11... | collective-permute-start | bytes 1179656 | tf_op jit(solution)/shard_map/ppermute | solution.py:338
  309.5 26.1 %all-to-all-start.2 = ((bf16[32,48,128]{2,1,0:T(8,128)(2,1)}), bf16[32,48,128]{2,1,0:T(8,128)(2,1)S(1)}, u32[]{:S(2)}, u32[]{:S(2)}) async-start(bf16[32,48,128]{2,1,0:T(8,128)(2,1)} %temporal.1), calls=%async_computation.2 | async-start | bytes 786432 | tf_op jit(solution)/shard_map/all_to_all | solution.py:391
  318.8 12.1 %collective-permute-start.22 = (bf16[4,192,256]{2,1,0:T(8,128)(2,1)}, bf16[4,192,256]{2,1,0:T(8,128)(2,1)S(1)}, u32[]{:S(2)}, u32[]{:S(2)}) collective-permute-start(bf16[4,192,256]{2,1,0:T(8,128)(2,1)} %get-tuple-element.29.refs_0_), channel_id=1, source_target_pairs={{0,2},{2,4},{4,6},{6,0},{1,3},{3,5},{5,7},{7,1},{8,10},{10,12},{12... | collective-permute-start | bytes 1179656 | tf_op jit(solution)/shard_map/ppermute | solution.py:338
  320.3 12.3 %collective-permute-start.25 = (bf16[4,192,256]{2,1,0:T(8,128)(2,1)}, bf16[4,192,256]{2,1,0:T(8,128)(2,1)S(1)}, u32[]{:S(2)}, u32[]{:S(2)}) collective-permute-start(bf16[4,192,256]{2,1,0:T(8,128)(2,1)} %collective-permute-done.21.refs_1_), channel_id=1, source_target_pairs={{0,6},{2,0},{4,2},{6,4},{1,7},{3,1},{5,3},{7,5},{8,14},{10,8},{12,... | collective-permute-start | bytes 1179656 | tf_op jit(solution)/shard_map/ppermute | solution.py:338
  322.1 19.0 %collective-permute-start.27 = (bf16[4,192,256]{2,1,0:T(8,128)(2,1)}, bf16[4,192,256]{2,1,0:T(8,128)(2,1)}, u32[]{:S(2)}, u32[]{:S(2)}) collective-permute-start(bf16[4,192,256]{2,1,0:T(8,128)(2,1)} %get-tuple-element.29.refs_0_), channel_id=1, source_target_pairs={{0,6},{2,0},{4,2},{6,4},{1,7},{3,1},{5,3},{7,5},{8,14},{10,8},{12,... | collective-permute-start | bytes 1179656 | tf_op jit(solution)/shard_map/ppermute | solution.py:338
  330.9 29.4 %copy-start.19 = (bf16[4,192,256]{2,1,0:T(8,128)(2,1)}, bf16[4,192,256]{2,1,0:T(8,128)(2,1)S(1)}, u32[]{:S(2)}) copy-start(bf16[4,192,256]{2,1,0:T(8,128)(2,1)S(1)} %collective-permute-done.22.refs_2_) | copy-start | bytes 1179652
  330.9 13.4 %collective-permute-start.24 = (bf16[4,192,256]{2,1,0:T(8,128)(2,1)S(1)}, bf16[4,192,256]{2,1,0:T(8,128)(2,1)}, u32[]{:S(2)}, u32[]{:S(2)}) collective-permute-start(bf16[4,192,256]{2,1,0:T(8,128)(2,1)S(1)} %collective-permute-done.22.refs_2_), channel_id=1, source_target_pairs={{0,2},{2,4},{4,6},{6,0},{1,3},{3,5},{5,7},{7,1},{8,10},{10,12},{12... | collective-permute-start | bytes 1179656 | tf_op jit(solution)/shard_map/ppermute | solution.py:338
  331.2 21.5 %collective-permute-start.23 = (bf16[4,192,256]{2,1,0:T(8,128)(2,1)}, bf16[4,192,256]{2,1,0:T(8,128)(2,1)}, u32[]{:S(2)}, u32[]{:S(2)}) collective-permute-start(bf16[4,192,256]{2,1,0:T(8,128)(2,1)} %collective-permute-done.21.refs_1_), channel_id=1, source_target_pairs={{0,2},{2,4},{4,6},{6,0},{1,3},{3,5},{5,7},{7,1},{8,10},{10,12},{12... | collective-permute-start | bytes 1179656 | tf_op jit(solution)/shard_map/ppermute | solution.py:338
  332.6 27.7 %copy-start.20 = (bf16[4,192,256]{2,1,0:T(8,128)(2,1)}, bf16[4,192,256]{2,1,0:T(8,128)(2,1)S(1)}, u32[]{:S(2)}) copy-start(bf16[4,192,256]{2,1,0:T(8,128)(2,1)S(1)} %collective-permute-done.25.refs_7_) | copy-start | bytes 1179652
  332.6 20.1 %collective-permute-start.26 = (bf16[4,192,256]{2,1,0:T(8,128)(2,1)S(1)}, bf16[4,192,256]{2,1,0:T(8,128)(2,1)}, u32[]{:S(2)}, u32[]{:S(2)}) collective-permute-start(bf16[4,192,256]{2,1,0:T(8,128)(2,1)S(1)} %collective-permute-done.25.refs_7_), channel_id=1, source_target_pairs={{0,6},{2,0},{4,2},{6,4},{1,7},{3,1},{5,3},{7,5},{8,14},{10,8},{12,... | collective-permute-start | bytes 1179656 | tf_op jit(solution)/shard_map/ppermute | solution.py:338
  335.6 81.3 %copy-start.3 = (bf16[16,48,128]{2,1,0:T(8,128)(2,1)}, bf16[16,48,128]{2,1,0:T(8,128)(2,1)S(1)}, u32[]{:S(2)}) copy-start(bf16[16,48,128]{2,1,0:T(8,128)(2,1)S(1)} %get-tuple-element.37.refs_1_) | copy-start | bytes 589828
  335.6 81.3 %copy-start.4 = (bf16[16,48,128]{2,1,0:T(8,128)(2,1)}, bf16[16,48,128]{2,1,0:T(8,128)(2,1)S(1)}, u32[]{:S(2)}) copy-start(bf16[16,48,128]{2,1,0:T(8,128)(2,1)S(1)} %get-tuple-element.38.refs_0_) | copy-start | bytes 589828
  341.1 15.7 %collective-permute-start.28 = (bf16[16,48,128]{2,1,0:T(8,128)(2,1)S(1)}, bf16[16,48,128]{2,1,0:T(8,128)(2,1)S(1)}, u32[]{:S(2)}, u32[]{:S(2)}) collective-permute-start(bf16[16,48,128]{2,1,0:T(8,128)(2,1)S(1)} %get-tuple-element.38.refs_0_), channel_id=1, source_target_pairs={{0,2},{2,4},{4,6},{6,0},{1,3},{3,5},{5,7},{7,1},{8,10},{10,12},{12... | collective-permute-start | bytes 589832 | tf_op jit(solution)/shard_map/ppermute | solution.py:338
  344.3 12.5 %collective-permute-start.31 = (bf16[16,48,128]{2,1,0:T(8,128)(2,1)S(1)}, bf16[16,48,128]{2,1,0:T(8,128)(2,1)S(1)}, u32[]{:S(2)}, u32[]{:S(2)}) collective-permute-start(bf16[16,48,128]{2,1,0:T(8,128)(2,1)S(1)} %get-tuple-element.37.refs_1_), channel_id=1, source_target_pairs={{0,6},{2,0},{4,2},{6,4},{1,7},{3,1},{5,3},{7,5},{8,14},{10,8},{12,... | collective-permute-start | bytes 589832 | tf_op jit(solution)/shard_map/ppermute | solution.py:338
  352.7 72.2 %collective-permute-start.29 = (bf16[16,48,128]{2,1,0:T(8,128)(2,1)S(1)}, bf16[16,48,128]{2,1,0:T(8,128)(2,1)S(1)}, u32[]{:S(2)}, u32[]{:S(2)}) collective-permute-start(bf16[16,48,128]{2,1,0:T(8,128)(2,1)S(1)} %get-tuple-element.37.refs_1_), channel_id=1, source_target_pairs={{0,2},{2,4},{4,6},{6,0},{1,3},{3,5},{5,7},{7,1},{8,10},{10,12},{12... | collective-permute-start | bytes 589832 | tf_op jit(solution)/shard_map/ppermute | solution.py:338
  352.7 72.2 %collective-permute-start.30 = (bf16[16,48,128]{2,1,0:T(8,128)(2,1)S(1)}, bf16[16,48,128]{2,1,0:T(8,128)(2,1)S(1)}, u32[]{:S(2)}, u32[]{:S(2)}) collective-permute-start(bf16[16,48,128]{2,1,0:T(8,128)(2,1)S(1)} %get-tuple-element.38.refs_0_), channel_id=1, source_target_pairs={{0,6},{2,0},{4,2},{6,4},{1,7},{3,1},{5,3},{7,5},{8,14},{10,8},{12,... | collective-permute-start | bytes 589832 | tf_op jit(solution)/shard_map/ppermute | solution.py:338
  356.8 60.1 %copy-start.10 = (bf16[16,48,128]{2,1,0:T(8,128)(2,1)}, bf16[16,48,128]{2,1,0:T(8,128)(2,1)S(1)}, u32[]{:S(2)}) copy-start(bf16[16,48,128]{2,1,0:T(8,128)(2,1)S(1)} %collective-permute-done.28.refs_0_) | copy-start | bytes 589828
  356.8 60.1 %collective-permute-start.34 = (bf16[16,48,128]{2,1,0:T(8,128)(2,1)S(1)}, bf16[16,48,128]{2,1,0:T(8,128)(2,1)S(1)}, u32[]{:S(2)}, u32[]{:S(2)}) collective-permute-start(bf16[16,48,128]{2,1,0:T(8,128)(2,1)S(1)} %collective-permute-done.28.refs_0_), channel_id=1, source_target_pairs={{0,2},{2,4},{4,6},{6,0},{1,3},{3,5},{5,7},{7,1},{8,10},{10,12},{12... | collective-permute-start | bytes 589832 | tf_op jit(solution)/shard_map/ppermute | solution.py:338
  356.8 60.1 %copy-start.11 = (bf16[16,48,128]{2,1,0:T(8,128)(2,1)}, bf16[16,48,128]{2,1,0:T(8,128)(2,1)S(1)}, u32[]{:S(2)}) copy-start(bf16[16,48,128]{2,1,0:T(8,128)(2,1)S(1)} %collective-permute-done.31.refs_3_) | copy-start | bytes 589828
  356.8 60.1 %collective-permute-start.35 = (bf16[16,48,128]{2,1,0:T(8,128)(2,1)S(1)}, bf16[16,48,128]{2,1,0:T(8,128)(2,1)S(1)}, u32[]{:S(2)}, u32[]{:S(2)}) collective-permute-start(bf16[16,48,128]{2,1,0:T(8,128)(2,1)S(1)} %collective-permute-done.31.refs_3_), channel_id=1, source_target_pairs={{0,6},{2,0},{4,2},{6,4},{1,7},{3,1},{5,3},{7,5},{8,14},{10,8},{12,... | collective-permute-start | bytes 589832 | tf_op jit(solution)/shard_map/ppermute | solution.py:338
  360.3 1.4 copy-start.18
  421.5 12.5 %collective-permute-start.36 = (bf16[96,768]{1,0:T(8,128)(2,1)}, bf16[96,768]{1,0:T(8,128)(2,1)S(1)}, u32[]{:S(2)}, u32[]{:S(2)}) collective-permute-start(bf16[96,768]{1,0:T(8,128)(2,1)} %get-tuple-element.35), channel_id=1, source_target_pairs={{0,2},{2,4},{4,6},{6,0},{1,3},{3,5},{5,7},{7,1},{8,10},{10,12},{12... | collective-permute-start | bytes 442376 | tf_op jit(solution)/shard_map/ppermute | solution.py:338
  421.6 12.4 %collective-permute-start.38 = (bf16[96,768]{1,0:T(8,128)(2,1)}, bf16[96,768]{1,0:T(8,128)(2,1)S(1)}, u32[]{:S(2)}, u32[]{:S(2)}) collective-permute-start(bf16[96,768]{1,0:T(8,128)(2,1)} %get-tuple-element.36), channel_id=1, source_target_pairs={{0,6},{2,0},{4,2},{6,4},{1,7},{3,1},{5,3},{7,5},{8,14},{10,8},{12,... | collective-permute-start | bytes 442376 | tf_op jit(solution)/shard_map/ppermute | solution.py:338
  430.7 10.4 %collective-permute-start.32 = (bf16[192,768]{1,0:T(8,128)(2,1)}, bf16[192,768]{1,0:T(8,128)(2,1)S(1)}, u32[]{:S(2)}, u32[]{:S(2)}) collective-permute-start(bf16[192,768]{1,0:T(8,128)(2,1)} %get-tuple-element.33), channel_id=1, source_target_pairs={{0,2},{2,4},{4,6},{6,0},{1,3},{3,5},{5,7},{7,1},{8,10},{10,12},{12... | collective-permute-start | bytes 884744 | tf_op jit(solution)/shard_map/ppermute | solution.py:338
  430.8 10.3 %collective-permute-start.33 = (bf16[192,768]{1,0:T(8,128)(2,1)}, bf16[192,768]{1,0:T(8,128)(2,1)S(1)}, u32[]{:S(2)}, u32[]{:S(2)}) collective-permute-start(bf16[192,768]{1,0:T(8,128)(2,1)} %get-tuple-element.34), channel_id=1, source_target_pairs={{0,6},{2,0},{4,2},{6,4},{1,7},{3,1},{5,3},{7,5},{8,14},{10,8},{12,... | collective-permute-start | bytes 884744 | tf_op jit(solution)/shard_map/ppermute | solution.py:338
  434.0 7.0 %collective-permute-start.37 = (bf16[96,768]{1,0:T(8,128)(2,1)S(1)}, bf16[96,768]{1,0:T(8,128)(2,1)S(1)}, u32[]{:S(2)}, u32[]{:S(2)}) collective-permute-start(bf16[96,768]{1,0:T(8,128)(2,1)S(1)} %collective-permute-done.36), channel_id=1, source_target_pairs={{0,2},{2,4},{4,6},{6,0},{1,3},{3,5},{5,7},{7,1},{8,10},{10,12},{12... | collective-permute-start | bytes 442376 | tf_op jit(solution)/shard_map/ppermute | solution.py:338
  434.0 7.1 %collective-permute-start.39 = (bf16[96,768]{1,0:T(8,128)(2,1)S(1)}, bf16[96,768]{1,0:T(8,128)(2,1)S(1)}, u32[]{:S(2)}, u32[]{:S(2)}) collective-permute-start(bf16[96,768]{1,0:T(8,128)(2,1)S(1)} %collective-permute-done.38), channel_id=1, source_target_pairs={{0,6},{2,0},{4,2},{6,4},{1,7},{3,1},{5,3},{7,5},{8,14},{10,8},{12,... | collective-permute-start | bytes 442376 | tf_op jit(solution)/shard_map/ppermute | solution.py:338
  (13 other events, 9.9 us)

commit v3 on v2

v3 whole, which is shorter than its diff:
```python
import jax
import jax.numpy as jnp
from jax import lax
from jax.experimental import pallas as pl
from jax.experimental.pallas import tpu as pltpu
from jax.sharding import Mesh, PartitionSpec as P

HEADS = 24
SIZE = 128
SPATIAL = 16
D = 3072
FRAMES = 32
ROWS = 192
RING = 4
SHARE = D // RING
GROUP = 48
EXP_SCALE = 1.4426950408889634 * SIZE ** -0.5
POS = ("y", "core")
BF16 = jnp.bfloat16
F32 = jnp.float32
SPATIAL_COST = 4_800_000_000
HALVE_COST = 40_000_000_000
COLLECT_COST = 40_000_000_000
VMEM = pl.BlockSpec(memory_space=pltpu.VMEM)
SMEM = pl.BlockSpec(memory_space=pltpu.SMEM)
ANY = pl.BlockSpec(memory_space=pl.ANY)


def shape(*dims, dtype=BF16):
    return jax.ShapeDtypeStruct(dims, dtype)


def params(mebibytes):
    return pltpu.CompilerParams(vmem_limit_bytes=mebibytes * 1024 * 1024)


def cost(flops, nbytes, exps=0):
    return pl.CostEstimate(flops=flops, bytes_accessed=nbytes, transcendentals=exps)


def rank_heads(kinds, ids):
    spatial_next, temporal_next = jnp.int32(0), jnp.int32(SPATIAL)
    for head in range(HEADS):
        kind = kinds[head]
        ids[jnp.where(kind == 0, spatial_next, temporal_next)] = head
        spatial_next, temporal_next = spatial_next + 1 - kind, temporal_next + kind


def head_columns(ids, rank):
    return pl.ds(pl.multiple_of(ids[rank] * SIZE, SIZE), SIZE)


def pack_spatial_kernel(kinds, qkv, *refs):
    outs, ids = refs[:8], refs[8]

    @pl.when(pl.program_id(0) == 0)
    def _():
        rank_heads(kinds, ids)

    y, core = lax.axis_index("y"), lax.axis_index("core")
    for part in range(2):
        for step in range(RING):
            to = lax.rem(y + step, RING) * 2 + lax.rem(core + part, 2)
            for head in range(2):
                outs[part * RING + step][0, head] = qkv[0, :, head_columns(ids, to * 2 + head)]


def pack_temporal_kernel(kinds, qkv, out, ids):
    @pl.when(pl.program_id(0) == 0)
    def _():
        rank_heads(kinds, ids)

    for head in range(HEADS - SPATIAL):
        columns = head_columns(ids, SPATIAL + head)
        for piece in range(RING):
            rows = slice(piece * GROUP, (piece + 1) * GROUP)
            out[head * RING + piece, 0] = qkv[0, rows, columns]


def pack_call(kernel, name, block, count):
    spec = pl.BlockSpec(
        (block[0], 1) + block[2:] if name == "pack_temporal" else (1,) + block[1:],
        (lambda c: (0, c, 0, 0)) if name == "pack_temporal" else (lambda c: (c, 0, 0, 0)),
    )
    return pl.pallas_call(
        kernel,
        grid=(3,),
        out_shape=[shape(*block)] * count,
        in_specs=[SMEM, pl.BlockSpec((1, ROWS, D), lambda c: (c, 0, 0))],
        out_specs=[spec] * count,
        scratch_shapes=[pltpu.SMEM((HEADS,), jnp.int32)],
        compiler_params=params(56),
        cost_estimate=cost(0, 4_800_000),
        name=name,
    )


def pack_spatial(kinds, qkv):
    return pack_call(pack_spatial_kernel, "pack_spatial", (3, 2, ROWS, SIZE), 8)(kinds, qkv)


def pack_temporal(kinds, qkv):
    return pack_call(pack_temporal_kernel, "pack_temporal", (FRAMES, 3, GROUP, SIZE), 1)(kinds, qkv)[0]


def attend(query, key, value_ones, keep=None):
    score = lax.dot_general(query, key, (((1,), (1,)), ((), ())), preferred_element_type=F32)
    if keep is not None:
        score = jnp.where(keep, score, -1e30)
    top = jnp.max(score, axis=1, keepdims=True)
    weight = jnp.exp2((score - top) * EXP_SCALE).astype(BF16)
    both = jnp.dot(weight, value_ones, preferred_element_type=F32)
    return (both[:, :SIZE] / both[:, SIZE:]).astype(BF16)


def spatial_kernel(*refs):
    chunks, outs = refs[:8], refs[8:]
    y = lax.axis_index("y")
    ones = jnp.ones((8 * ROWS, SIZE), BF16)
    for head in range(2):
        key = jnp.concatenate([chunk[1, head] for chunk in chunks], axis=0)
        value = jnp.concatenate([chunk[2, head] for chunk in chunks], axis=0)
        value_ones = jnp.concatenate([value, ones], axis=1)
        for pair in range(4):
            two = (pair * 2, pair * 2 + 1)
            query = jnp.concatenate([chunks[i][0, head] for i in two], axis=0)
            result = attend(query, key, value_ones)
            for n, i in enumerate(two):
                origin = lax.rem(y + RING - i % RING, RING)
                outs[i // RING][origin, :, head * SIZE : (head + 1) * SIZE] = result[
                    n * ROWS : (n + 1) * ROWS
                ]


def spatial(chunks):
    return pl.pallas_call(
        spatial_kernel,
        out_shape=[shape(RING, ROWS, 2 * SIZE)] * 2,
        in_specs=[VMEM] * 8,
        out_specs=[VMEM] * 2,
        compiler_params=params(24),
        cost_estimate=cost(SPATIAL_COST, 4_000_000, 4_700_000),
        name="spatial",
    )(*chunks)


def temporal_kernel(heads, _, out):
    span = 16
    count = FRAMES * span
    same = lax.broadcasted_iota(jnp.int32, (count, count), 0) % span == (
        lax.broadcasted_iota(jnp.int32, (count, count), 1) % span
    )
    ones = jnp.ones((count, SIZE), BF16)
    for piece in range(GROUP // span):
        rows = slice(piece * span, (piece + 1) * span)
        query, key, value = (heads[:, c, rows].reshape(count, SIZE) for c in range(3))
        result = attend(query, key, jnp.concatenate([value, ones], axis=1), same)
        out[:, rows] = result.reshape(FRAMES, span, SIZE)


def temporal(heads, done):
    return pl.pallas_call(
        temporal_kernel,
        out_shape=shape(FRAMES, GROUP, SIZE),
        in_specs=[VMEM, ANY],
        out_specs=VMEM,
        compiler_params=params(16),
        cost_estimate=cost(600_000_000, 1_600_000, 800_000),
        name="temporal",
    )(heads, done)


def after(arrays, done):
    def kernel(*refs):
        for i in range(len(arrays)):
            refs[len(arrays) + 1 + i][...] = refs[i][...]

    return pl.pallas_call(
        kernel,
        out_shape=[shape(*array.shape) for array in arrays],
        in_specs=[VMEM] * len(arrays) + [ANY],
        out_specs=[VMEM] * len(arrays),
        compiler_params=params(4),
        cost_estimate=cost(0, 300_000),
        name="after",
    )(*arrays, done)


def join3_kernel(first, second, third, _, out):
    for i, ref in enumerate((first, second, third)):
        out[i] = ref[...]


def join3(slabs, done):
    return pl.pallas_call(
        join3_kernel,
        out_shape=shape(3, *slabs[0].shape),
        in_specs=[VMEM] * 3 + [ANY],
        out_specs=VMEM,
        compiler_params=params(4),
        cost_estimate=cost(0, 400_000),
        name="join3",
    )(*slabs, done)


def join8_kernel(near, behind, ahead, _, out):
    z = lax.axis_index("z")
    for i in range(3):
        out[lax.rem(z + 7 + i, 8)] = near[i]
        out[lax.rem(z + 4 + i, 8)] = behind[i]
    for i in range(2):
        out[lax.rem(z + 2 + i, 8)] = ahead[i]


def join8(near, behind, ahead, done):
    return pl.pallas_call(
        join8_kernel,
        out_shape=shape(8, *near.shape[1:]),
        in_specs=[VMEM] * 3 + [ANY],
        out_specs=VMEM,
        compiler_params=params(4),
        cost_estimate=cost(0, 1_200_000),
        name="join8",
    )(near, behind, ahead, done)


def arrange_kernel(own, behind, far, ahead, out):
    x = lax.axis_index("x")
    for step, block in enumerate((own, behind, far, ahead)):
        x_from = lax.rem(x + RING - step, RING)
        for z in range(8):
            out[z * RING + x_from] = block[z]


def arrange(*blocks):
    return pl.pallas_call(
        arrange_kernel,
        out_shape=shape(FRAMES, 96, SHARE // 2),
        in_specs=[VMEM] * 4,
        out_specs=VMEM,
        compiler_params=params(12),
        cost_estimate=cost(0, 4_800_000),
        name="arrange",
    )(*blocks)


def halve_kernel(whole, low, high):
    low[...] = whole[:16]
    high[...] = whole[16:]


def halve(whole):
    return pl.pallas_call(
        halve_kernel,
        out_shape=[shape(16, GROUP, SIZE)] * 2,
        in_specs=[VMEM],
        out_specs=[VMEM] * 2,
        compiler_params=params(4),
        cost_estimate=cost(HALVE_COST, 800_000),
        name="halve",
    )(whole)


def collect_kernel(*refs):
    for slot in range(8):
        refs[8][:, :, slot * 256 : (slot + 1) * 256] = refs[slot][...]


def collect(blocks):
    return pl.pallas_call(
        collect_kernel,
        out_shape=shape(RING, ROWS, SPATIAL * SIZE),
        in_specs=[VMEM] * 8,
        out_specs=VMEM,
        compiler_params=params(12),
        cost_estimate=cost(COLLECT_COST, 6_400_000),
        name="collect",
    )(*blocks)


def project_spatial_kernel(kinds, weight_own, weight_other, tokens, total, weight_temporal, ids, held):
    y, core = lax.axis_index("y"), lax.axis_index("core")
    rank_heads(kinds, ids)
    ranks = []
    for step in range(RING):
        origin = lax.rem(y + RING - step, RING)
        for part in range(2):
            first = origin * 4 + lax.rem(core + part, 2) * 2
            ranks += [first, first + 1]
    left = tokens[...].reshape(RING * ROWS, SPATIAL * SIZE)
    for part, half in enumerate((weight_own, weight_other)):
        start = pl.multiple_of(lax.rem(core + part, 2) * (SHARE // 2), SIZE)
        columns = pl.ds(start, SHARE // 2)
        for slot, rank in enumerate(ranks):
            held[slot * SIZE : (slot + 1) * SIZE] = half[head_columns(ids, rank)]
        for head in range(HEADS - SPATIAL):
            rows = slice(head * SIZE, (head + 1) * SIZE)
            weight_temporal[rows, columns] = half[head_columns(ids, SPATIAL + head)]
        product = jnp.dot(left, held[...], preferred_element_type=F32)
        total[:, :, columns] = product.reshape(RING, ROWS, SHARE // 2)


def project_spatial(kinds, weight_own, weight_other, tokens):
    return pl.pallas_call(
        project_spatial_kernel,
        out_shape=[shape(RING, ROWS, SHARE, dtype=F32), shape(D - SPATIAL * SIZE, SHARE)],
        in_specs=[SMEM] + [VMEM] * 3,
        out_specs=[VMEM, VMEM],
        scratch_shapes=[
            pltpu.SMEM((HEADS,), jnp.int32),
            pltpu.VMEM((SPATIAL * SIZE, SHARE // 2), BF16),
        ],
        compiler_params=params(32),
        cost_estimate=cost(2_400_000_000, 11_000_000),
        name="project_spatial",
    )(kinds, weight_own, weight_other, tokens)


def project_temporal_kernel(total, weight, *refs):
    ins, out = refs[:8], refs[8]
    y = lax.axis_index("y")
    for step in range(RING):
        origin = lax.rem(y + RING - step, RING)
        heads = []
        for half in ins[2 * step : 2 * step + 2]:
            heads += [half[h * 4 : h * 4 + 4].reshape(ROWS, SIZE) for h in range(4)]
        left = jnp.concatenate(heads, axis=1)
        product = jnp.dot(left, weight[...], preferred_element_type=F32)
        out[origin] = (total[origin] + product).astype(BF16)


def project_temporal(total, weight, halves):
    return pl.pallas_call(
        project_temporal_kernel,
        out_shape=shape(RING, ROWS, SHARE),
        in_specs=[VMEM] * 10,
        out_specs=VMEM,
        compiler_params=params(24),
        cost_estimate=cost(1_200_000_000, 7_000_000),
        name="project_temporal",
    )(total, weight, *halves)


def finish_kernel(blocks, out):
    for y in range(RING):
        out[:, y * SHARE : (y + 1) * SHARE] = blocks[y]


def finish(blocks):
    return pl.pallas_call(
        finish_kernel,
        out_shape=shape(ROWS, D),
        in_specs=[VMEM],
        out_specs=VMEM,
        compiler_params=params(8),
        cost_estimate=cost(0, 2_400_000),
        name="finish",
    )(blocks)


def hop(array, axis, steps):
    size = lax.axis_size(axis)
    return lax.ppermute(array, axis, [(i, (i + steps) % size) for i in range(size)])


def hop_over(array, steps):
    perm = [
        (y * 2 + core, ((y + steps) % RING) * 2 + 1 - core)
        for y in range(RING)
        for core in range(2)
    ]
    return lax.ppermute(array, POS, perm)


def weight_slab(out_weight):
    sent = jnp.transpose(out_weight.reshape(12, 8, SHARE // 2), (1, 0, 2))
    return lax.all_to_all(sent, POS, 0, 0, tiled=True).reshape(96, SHARE // 2)


def shards(qkv, head_kind, out_weight):
    qkv = qkv.reshape(3, ROWS, D)
    slab = weight_slab(out_weight)
    across = lax.all_to_all(pack_temporal(head_kind, qkv), ("z", "x"), 0, 0, tiled=True)
    packed = pack_spatial(head_kind, qkv)
    far_same, far_cross = hop(packed[2], "y", 1), hop(packed[6], "y", -1)
    chunks = [
        packed[0],
        hop(packed[1], "y", 1),
        hop(far_same, "y", 1),
        hop(packed[3], "y", -1),
        hop(packed[4], "core", 1),
        hop_over(packed[5], 1),
        hop_over(far_cross, -1),
        hop_over(packed[7], -1),
    ]
    (slab,) = after([slab], far_same)
    near = join3([hop(slab, "z", 1), slab, hop(slab, "z", -1)], chunks[2])
    near_behind, near_ahead = hop(near, "z", 3), hop(near, "z", -3)

    mine, other = spatial(chunks)
    theirs = hop(other, "core", 1)
    mine_behind, mine_ahead = hop(mine, "y", 1), hop(mine, "y", -1)
    theirs_behind, theirs_ahead = hop(theirs, "y", 1), hop(theirs, "y", -1)
    mine_far = hop(mine_behind, "y", 1)
    theirs_far = hop(theirs_ahead, "y", -1)

    slabs = join8(near, near_behind, near_ahead, mine)
    w_behind, w_ahead = hop(slabs, "x", 1), hop(slabs, "x", -1)
    w_far = hop(w_behind, "x", 1)
    weight_own = arrange(slabs, w_behind, w_far, w_ahead).reshape(D, SHARE // 2)
    weight_other = hop(weight_own, "core", 1)

    back = lax.all_to_all(temporal(across, mine_behind), ("z", "x"), 0, 0, tiled=True)
    low, high = halve(back)
    low_behind, high_ahead = hop(low, "y", 1), hop(high, "y", -1)
    high_behind, low_ahead = hop(high, "y", 1), hop(low, "y", -1)
    low_far, high_far = hop(low_behind, "y", 1), hop(high_ahead, "y", -1)

    blocks = [mine, theirs, mine_behind, theirs_behind, mine_far, theirs_far, mine_ahead, theirs_ahead]
    total, weight_temporal = project_spatial(head_kind, weight_own, weight_other, collect(blocks))
    halves = [low, high, low_behind, high_behind, low_far, high_far, low_ahead, high_ahead]
    out = project_temporal(total, weight_temporal, halves)
    return finish(lax.all_to_all(out, "y", 0, 0, tiled=True)).reshape(1, ROWS, D)


def solution(mesh):
    split = Mesh(mesh.devices.reshape(8, 4, 4, 2), ("z", "x", "y", "core"))
    placed = (P(None, ("z", "x"), POS, None), P(), P(("z", "x", "y", "core"), None))
    return jax.shard_map(
        shards, mesh=split, in_specs=placed, out_specs=P(("z", "x"), POS, None), check_vma=False
    )
```

time: 489 us -> 159 us (0.33); the launches traced: 480 us -> 156 us
  Pallas kernels: 300 us -> 28.8 us
  waiting for transfers between devices: 91.8 us -> 48.9 us
  starting transfers between devices: 77.1 us -> 61.5 us
  blocking collectives: 0 us -> 14.3 us
  local copies, waits for them, and re-layouts: 10.1 us -> 2.54 us
    pallas_call x6 -> x9, Pallas kernels: 160 us -> 14.4 us  [the longest x1 4.59 us: pack_spatial(): pack_call(pack_spatial_kernel, 'pack_spatial', (3, 2, ROWS, SIZE), 8)]
    pallas_call x1, Pallas kernels: 72.9 us -> 0.22 us  [arrange(): pl.pallas_call(arrange_kernel, out_shape=shape(FRAMES, 96, SHARE // 2), i...]
    pallas_call x1, Pallas kernels: 55.2 us -> 5.45 us  [project_spatial(): pl.pallas_call(project_spatial_kernel, out_shape=[shape(RING, ROWS, SHARE...]
    ppermute x37 -> x27, waiting for transfers between devices: 86.9 us -> 43.5 us  [hop(): lax.ppermute(array, axis, [(i, (i + steps) % size) for i in range(size)])]
    ppermute x37 -> x27, starting transfers between devices: 50.5 us -> 34 us  [hop(): lax.ppermute(array, axis, [(i, (i + steps) % size) for i in range(size)])]
    all_to_all x0 -> x1, blocking collectives: none -> 14.3 us  [shards(): lax.all_to_all(out, 'y', 0, 0, tiled=True)]
    unnamed x76 -> x5, local copies, waits for them, and re-layouts: 9.25 us -> 1.87 us
  transfers between devices with their start and end apart: 43 -> 33, of which waited for: 18 -> 11; matrix products, arithmetic and copies ran while one was open for 0% -> 0% of each run, Pallas kernels for 55% -> 17%
where the time goes in v3:
time: 159 us; the launch traced here: 156 us
  starting transfers between devices  61.5 us (39%)
  waiting for transfers between devices  48.9 us (31%)
  Pallas kernels  28.8 us (18%)
  blocking collectives  14.3 us (9%)
  local copies, waits for them, and re-layouts  2.54 us (2%)
    ppermute x27, waiting for transfers between devices, hop(): lax.ppermute(array, axis, [(i, (i + steps) % size) for i in range(size)])  43.5 us
    ppermute x27, starting transfers between devices, hop(): lax.ppermute(array, axis, [(i, (i + steps) % size) for i in range(size)])  34 us
    all_to_all x1, blocking collectives, shards(): lax.all_to_all(out, 'y', 0, 0, tiled=True)  14.3 us
    all_to_all x1, starting transfers between devices, shards(): lax.all_to_all(pack_temporal(head_kind, qkv), ('z', 'x'), 0, 0, tiled=True)  11.6 us
    all_to_all x1, starting transfers between devices, shards(): lax.all_to_all(temporal(across, mine_behind), ('z', 'x'), 0, 0, tiled=True)  8.42 us
    pallas_call x1, Pallas kernels, spatial(): pl.pallas_call(spatial_kernel, out_shape=[shape(RING, ROWS, 2 * SIZE)] *...  6.6 us
    pallas_call x1, Pallas kernels, project_spatial(): pl.pallas_call(project_spatial_kernel, out_shape=[shape(RING, ROWS, SHARE...  5.45 us
    pallas_call x1, Pallas kernels, pack_spatial(): pack_call(pack_spatial_kernel, 'pack_spatial', (3, 2, ROWS, SIZE), 8)  4.59 us
  transfers between devices with their start and end apart: 33, of which 11 were waited for; matrix products, arithmetic and copies ran while one was open for 0% of the time, Pallas kernels for 17%

profile of v3, /device:TPU:2, one launch (start us, length us, event | category | flops | bytes accessed | tf_op | source)
XLA Modules:
  0.0 156.2 jit_solution(7934947994806329429)
XLA Ops:
  0.0 0.9 copy.6
  0.9 0.6 copy.8
  1.6 4.5 %all-to-all-start = ((bf16[8,12,384]{2,1,0:T(8,128)(2,1)}), bf16[8,12,384]{2,1,0:T(8,128)(2,1)S(1)}, u32[]{:S(2)}, u32[]{:S(2)}) async-start(bf16[8,12,384]{2,1,0:T(8,128)(2,1)} %bitcast.8), calls=%async_computation | async-start | bytes 196608 | tf_op jit(solution)/shard_map/all_to_all | solution.py:377
  6.0 3.9 %pack_temporal.1 = bf16[32,3,48,128]{3,2,1,0:T(8,128)(2,1)} custom-call(s32[24]{0:T(128)} %kinds.5, bf16[3,192,3072]{2,1,0:T(8,128)(2,1)} %bitcast.11), custom_call_target="tpu_custom_call" | custom-call | bytes 4800000 | tf_op jit(solution)/shard_map/pack_temporal/pallas_call | solution.py:103
  10.0 1.9 %all-to-all-done = bf16[8,12,384]{2,1,0:T(8,128)(2,1)S(1)} async-done(((bf16[8,12,384]{2,1,0:T(8,128)(2,1)}), bf16[8,12,384]{2,1,0:T(8,128)(2,1)S(1)}, u32[]{:S(2)}, u32[]{:S(2)}) %all-to-all-start) | async-done | bytes 73760 | tf_op jit(solution)/shard_map/all_to_all | solution.py:377
  11.8 11.6 %all-to-all-start.1 = ((bf16[32,3,48,128]{3,2,1,0:T(8,128)(2,1)}), bf16[32,3,48,128]{3,2,1,0:T(8,128)(2,1)S(1)}, u32[]{:S(2)}, u32[]{:S(2)}) async-start(bf16[32,3,48,128]{3,2,1,0:T(8,128)(2,1)} %pack_temporal.1), calls=%async_computation.1 | async-start | bytes 2359296 | tf_op jit(solution)/shard_map/all_to_all | solution.py:383
  23.5 4.6 %pack_spatial.1 = (bf16[3,2,192,128]{3,2,1,0:T(8,128)(2,1)}, bf16[3,2,192,128]{3,2,1,0:T(8,128)(2,1)}, bf16[3,2,192,128]{3,2,1,0:T(8,128)(2,1)}, bf16[3,2,192,12...) custom-call(s32[24]{0:T(128)} %kinds.5, ...), custom_call_target="tpu_custom_call" | custom-call | bytes 4800000 | tf_op jit(solution)/shard_map/pack_spatial/pallas_call | solution.py:99
  28.0 0.6 collective-permute-start
  28.6 2.7 %collective-permute-start.10 = (bf16[3,2,192,128]{3,2,1,0:T(8,128)(2,1)}, bf16[3,2,192,128]{3,2,1,0:T(8,128)(2,1)S(1)}, u32[]{:S(2)}, u32[]{:S(2)}) collective-permute-start(bf16[3,2,192,128]{3,2,1,0:T(8,128)(2,1)} %get-tuple-element.25), channel_id=1, source_target_pairs={{0,6},{2,0},{4,2},{6,4},{1,7},{3,1},{5,3},{7,5},{8,14},{10,8},{12,... | collective-permute-start | bytes 884744 | tf_op jit(solution)/shard_map/ppermute | solution.py:363
  31.3 6.2 %collective-permute-done.refs_1_ = bf16[3,2,192,128]{3,2,1,0:T(8,128)(2,1)S(1)} collective-permute-done((bf16[3,2,192,128]{3,2,1,0:T(8,128)(2,1)}, bf16[3,2,192,128]{3,2,1,0:T(8,128)(2,1)S(1)}, u32[]{:S(2)}, u32[]{:S(2)}) %collective-permute-start) | collective-permute-done | bytes 294944 | tf_op jit(solution)/shard_map/ppermute | solution.py:363
  37.6 1.5 collective-permute-start.1
  39.1 1.8 %collective-permute-start.2 = (bf16[96,384]{1,0:T(8,128)(2,1)S(1)}, bf16[96,384]{1,0:T(8,128)(2,1)S(1)}, u32[]{:S(2)}, u32[]{:S(2)}) collective-permute-start(bf16[96,384]{1,0:T(8,128)(2,1)S(1)} %after.1.second), channel_id=1, source_target_pairs={{0,224},{32,0},{64,32},{96,64},{128,96},{160,128},{192,160},{224,1... | collective-permute-start | bytes 221192 | tf_op jit(solution)/shard_map/ppermute | solution.py:363
  40.9 0.9 collective-permute-start.6
  41.8 1.5 collective-permute-done.12.refs_7_
  43.2 1.4 collective-permute-start.7
  44.6 7.7 %collective-permute-done.1.first = bf16[96,384]{1,0:T(8,128)(2,1)S(1)} collective-permute-done((bf16[96,384]{1,0:T(8,128)(2,1)S(1)}, bf16[96,384]{1,0:T(8,128)(2,1)S(1)}, u32[]{:S(2)}, u32[]{:S(2)}) %collective-permute-start.1) | collective-permute-done | bytes 73760 | tf_op jit(solution)/shard_map/ppermute | solution.py:363
  52.4 0.7 collective-permute-start.9
  53.1 0.0 collective-permute-done.3._.refs_2_
  53.1 2.2 %collective-permute-start.11 = (bf16[3,2,192,128]{3,2,1,0:T(8,128)(2,1)S(1)}, bf16[3,2,192,128]{3,2,1,0:T(8,128)(2,1)S(1)}, u32[]{:S(2)}, u32[]{:S(2)}) collective-permute-start(bf16[3,2,192,128]{3,2,1,0:T(8,128)(2,1)S(1)} %collective-permute-done.10), channel_id=1, source_target_pairs={{0,7},{1,6},{2,1},{3,0},{4,3},{5,2},{6,5},{7,4},{8,15},{9,14},{10,... | collective-permute-start | bytes 884744 | tf_op jit(solution)/shard_map/ppermute | solution.py:372
  55.3 0.0 collective-permute-done.6.refs_1_
  55.4 4.0 %collective-permute-start.4 = (bf16[3,96,384]{2,1,0:T(8,128)(2,1)S(1)}, bf16[3,96,384]{2,1,0:T(8,128)(2,1)S(1)}, u32[]{:S(2)}, u32[]{:S(2)}) collective-permute-start(bf16[3,96,384]{2,1,0:T(8,128)(2,1)S(1)} %join3.1.near), channel_id=1, source_target_pairs={{0,96},{32,128},{64,160},{96,192},{128,224},{160,0},{192,32},{224,... | collective-permute-start | bytes 663560 | tf_op jit(solution)/shard_map/ppermute | solution.py:363
  59.4 0.0 collective-permute-done.7.refs_3_
  59.4 1.1 collective-permute-start.5
  60.5 2.0 %collective-permute-done.9.refs_5_ = bf16[3,2,192,128]{3,2,1,0:T(8,128)(2,1)S(1)} collective-permute-done((bf16[3,2,192,128]{3,2,1,0:T(8,128)(2,1)}, bf16[3,2,192,128]{3,2,1,0:T(8,128)(2,1)S(1)}, u32[]{:S(2)}, u32[]{:S(2)}) %collective-permute-start.9) | collective-permute-done | bytes 294944 | tf_op jit(solution)/shard_map/ppermute | solution.py:372
  62.4 0.1 collective-permute-done.11.refs_6_
  62.5 1.0 copy-done.1
  63.5 6.6 %spatial.1 = (bf16[4,192,256]{2,1,0:T(8,128)(2,1)}, bf16[4,192,256]{2,1,0:T(8,128)(2,1)S(1)}) custom-call(bf16[3,2,192,128]{3,2,1,0:T(8,128)(2,1)S(1)} %copy-done.1, bf16[3,2,192,128]{3,2,1,0:T(8,128)(2,1)S(1)} %collective-permute-done.6.refs_1_, bf16[3,2,192,128]{3,2,1,0:T(8,128)(2,1)S(1)} %collective-permute-done.3._.refs_2_, ...), custom_call_target="tpu_custom_call" | custom-call | flops 4800000000 | bytes 4000000 | tf_op jit(solution)/shard_map/spatial/pallas_call | solution.py:136
  70.1 1.2 collective-permute-start.18
  71.3 3.4 %collective-permute-done.4.behind = bf16[3,96,384]{2,1,0:T(8,128)(2,1)S(1)} collective-permute-done((bf16[3,96,384]{2,1,0:T(8,128)(2,1)S(1)}, bf16[3,96,384]{2,1,0:T(8,128)(2,1)S(1)}, u32[]{:S(2)}, u32[]{:S(2)}) %collective-permute-start.4) | collective-permute-done | bytes 221216 | tf_op jit(solution)/shard_map/ppermute | solution.py:363
  74.7 0.0 collective-permute-done.5.ahead
  74.7 0.1 join8.1.own
  74.8 1.7 %collective-permute-start.13 = (bf16[8,96,384]{2,1,0:T(8,128)(2,1)S(1)}, bf16[8,96,384]{2,1,0:T(8,128)(2,1)S(1)}, u32[]{:S(2)}, u32[]{:S(2)}) collective-permute-start(bf16[8,96,384]{2,1,0:T(8,128)(2,1)S(1)} %join8.1.own), channel_id=1, source_target_pairs={{0,8},{8,16},{16,24},{24,0},{1,9},{9,17},{17,25},{25,1},{2,10},{10... | collective-permute-start | bytes 1769480 | tf_op jit(solution)/shard_map/ppermute | solution.py:363
  76.5 7.0 %collective-permute-done.18.refs_2_._ = bf16[4,192,256]{2,1,0:T(8,128)(2,1)} collective-permute-done((bf16[4,192,256]{2,1,0:T(8,128)(2,1)}, bf16[4,192,256]{2,1,0:T(8,128)(2,1)}, u32[]{:S(2)}, u32[]{:S(2)}) %collective-permute-start.18) | collective-permute-done | bytes 393248 | tf_op jit(solution)/shard_map/ppermute | solution.py:363
  83.5 2.1 %temporal.1 = bf16[32,48,128]{2,1,0:T(8,128)(2,1)} custom-call(bf16[32,3,48,128]{3,2,1,0:T(8,128)(2,1)S(1)} %all-to-all-done.1.heads, bf16[4,192,256]{2,1,0:T(8,128)(2,1)} %collective-permute-done.18.refs_2_._), custom_call_target="tpu_custom_call" | custom-call | flops 600000000 | bytes 1600000 | tf_op jit(solution)/shard_map/temporal/pallas_call | solution.py:162
  85.6 8.4 %all-to-all-start.2 = ((bf16[32,48,128]{2,1,0:T(8,128)(2,1)}), bf16[32,48,128]{2,1,0:T(8,128)(2,1)}, u32[]{:S(2)}, u32[]{:S(2)}) async-start(bf16[32,48,128]{2,1,0:T(8,128)(2,1)} %temporal.1), calls=%async_computation.2 | async-start | bytes 786432 | tf_op jit(solution)/shard_map/all_to_all | solution.py:413
  94.1 0.4 collective-permute-start.15
  94.4 1.7 %collective-permute-start.14 = (bf16[8,96,384]{2,1,0:T(8,128)(2,1)S(1)}, bf16[8,96,384]{2,1,0:T(8,128)(2,1)S(1)}, u32[]{:S(2)}, u32[]{:S(2)}) collective-permute-start(bf16[8,96,384]{2,1,0:T(8,128)(2,1)S(1)} %collective-permute-done.13.behind), channel_id=1, source_target_pairs={{0,8},{8,16},{16,24},{24,0},{1,9},{9,17},{17,25},{25,1},{2,10},{10... | collective-permute-start | bytes 1769480 | tf_op jit(solution)/shard_map/ppermute | solution.py:363
  96.2 1.7 %collective-permute-start.21 = (bf16[4,192,256]{2,1,0:T(8,128)(2,1)}, bf16[4,192,256]{2,1,0:T(8,128)(2,1)}, u32[]{:S(2)}, u32[]{:S(2)}) collective-permute-start(bf16[4,192,256]{2,1,0:T(8,128)(2,1)} %collective-permute-done.17.refs_1_), channel_id=1, source_target_pairs={{0,6},{2,0},{4,2},{6,4},{1,7},{3,1},{5,3},{7,5},{8,14},{10,8},{12,... | collective-permute-start | bytes 1179656 | tf_op jit(solution)/shard_map/ppermute | solution.py:363
  97.9 0.0 collective-permute-start.23
  98.0 2.0 %collective-permute-start.20 = (bf16[4,192,256]{2,1,0:T(8,128)(2,1)}, bf16[4,192,256]{2,1,0:T(8,128)(2,1)}, u32[]{:S(2)}, u32[]{:S(2)}) collective-permute-start(bf16[4,192,256]{2,1,0:T(8,128)(2,1)} %collective-permute-done.18.refs_2_._), channel_id=1, source_target_pairs={{0,2},{2,4},{4,6},{6,0},{1,3},{3,5},{5,7},{7,1},{8,10},{10,12},{12... | collective-permute-start | bytes 1179656 | tf_op jit(solution)/shard_map/ppermute | solution.py:363
  99.9 8.6 %collective-permute-done.21.refs_7_ = bf16[4,192,256]{2,1,0:T(8,128)(2,1)} collective-permute-done((bf16[4,192,256]{2,1,0:T(8,128)(2,1)}, bf16[4,192,256]{2,1,0:T(8,128)(2,1)}, u32[]{:S(2)}, u32[]{:S(2)}) %collective-permute-start.21) | collective-permute-done | bytes 393248 | tf_op jit(solution)/shard_map/ppermute | solution.py:363
  108.5 4.2 %collective-permute-done.15.ahead = bf16[8,96,384]{2,1,0:T(8,128)(2,1)S(1)} collective-permute-done((bf16[8,96,384]{2,1,0:T(8,128)(2,1)S(1)}, bf16[8,96,384]{2,1,0:T(8,128)(2,1)S(1)}, u32[]{:S(2)}, u32[]{:S(2)}) %collective-permute-start.15) | collective-permute-done | bytes 589856 | tf_op jit(solution)/shard_map/ppermute | solution.py:363
  112.7 1.4 collective-permute-start.22
  114.2 0.2 arrange.1
  114.4 0.1 collective-permute-start.16
  114.5 0.0 all-to-all-done.2.whole
  114.5 1.0 halve.1
  115.5 0.0 collective-permute-done.23.refs_6_
  115.5 0.7 collective-permute-start.24
  116.2 0.0 collective-permute-done.20.refs_4_
  116.2 2.6 %collective-permute-start.27 = (bf16[16,48,128]{2,1,0:T(8,128)(2,1)S(1)}, bf16[16,48,128]{2,1,0:T(8,128)(2,1)S(1)}, u32[]{:S(2)}, u32[]{:S(2)}) collective-permute-start(bf16[16,48,128]{2,1,0:T(8,128)(2,1)S(1)} %get-tuple-element.32.refs_1_), channel_id=1, source_target_pairs={{0,6},{2,0},{4,2},{6,4},{1,7},{3,1},{5,3},{7,5},{8,14},{10,8},{12,... | collective-permute-start | bytes 589832 | tf_op jit(solution)/shard_map/ppermute | solution.py:363
  118.8 0.0 collective-permute-done.19.refs_3_
  118.8 6.2 %collective-permute-done.22.refs_5_ = bf16[4,192,256]{2,1,0:T(8,128)(2,1)} collective-permute-done((bf16[4,192,256]{2,1,0:T(8,128)(2,1)}, bf16[4,192,256]{2,1,0:T(8,128)(2,1)}, u32[]{:S(2)}, u32[]{:S(2)}) %collective-permute-start.22) | collective-permute-done | bytes 393248 | tf_op jit(solution)/shard_map/ppermute | solution.py:363
  125.1 2.2 %collect.1.tokens = bf16[4,192,2048]{2,1,0:T(8,128)(2,1)S(1)} custom-call(bf16[4,192,256]{2,1,0:T(8,128)(2,1)} %get-tuple-element.27._.refs_0_, bf16[4,192,256]{2,1,0:T(8,128)(2,1)} %collective-permute-done.17.refs_1_, bf16[4,192,256]{2,1,0:T(8,128)(2,1)} %collective-permute-done.18.refs_2_._, bf16[4,192,256]{2,1,0:T(8,128)(2,1)} %collective-permute-done.19.refs_3_, ...), custom_call_target="tpu_custom_call" | custom-call | flops 40000000000 | bytes 6400000 | tf_op jit(solution)/shard_map/collect/pallas_call | solution.py:270
  127.3 0.1 collective-permute-start.25
  127.4 3.2 %collective-permute-start.29 = (bf16[16,48,128]{2,1,0:T(8,128)(2,1)S(1)}, bf16[16,48,128]{2,1,0:T(8,128)(2,1)S(1)}, u32[]{:S(2)}, u32[]{:S(2)}) collective-permute-start(bf16[16,48,128]{2,1,0:T(8,128)(2,1)S(1)} %get-tuple-element.31.refs_0_), channel_id=1, source_target_pairs={{0,6},{2,0},{4,2},{6,4},{1,7},{3,1},{5,3},{7,5},{8,14},{10,8},{12,... | collective-permute-start | bytes 589832 | tf_op jit(solution)/shard_map/ppermute | solution.py:363
  130.7 0.0 collective-permute-done.24.refs_2_
  130.7 0.0 collective-permute-start.26
  130.7 0.0 collective-permute-done.27.refs_7_
  130.7 3.2 %collective-permute-start.28 = (bf16[16,48,128]{2,1,0:T(8,128)(2,1)S(1)}, bf16[16,48,128]{2,1,0:T(8,128)(2,1)S(1)}, u32[]{:S(2)}, u32[]{:S(2)}) collective-permute-start(bf16[16,48,128]{2,1,0:T(8,128)(2,1)S(1)} %collective-permute-done.27.refs_7_), channel_id=1, source_target_pairs={{0,6},{2,0},{4,2},{6,4},{1,7},{3,1},{5,3},{7,5},{8,14},{10,8},{12,... | collective-permute-start | bytes 589832 | tf_op jit(solution)/shard_map/ppermute | solution.py:363
  133.9 5.5 %project_spatial.1 = (f32[4,192,768]{2,1,0:T(8,128)S(1)}, bf16[1024,768]{1,0:T(8,128)(2,1)S(1)}) custom-call(s32[24]{0:T(128)S(1)} %copy-done, bf16[3072,384]{1,0:T(8,128)(2,1)S(1)} %bitcast.10, bf16[3072,384]{1,0:T(8,128)(2,1)} %collective-permute-done.16.weight_other, bf16[4,192,2048]{2,1,0:T(8,128)(2,1)S(1)} %collect.1.tokens), custom_call_target="tpu_custom_call" | custom-call | flops 2400000000 | bytes 11000000 | tf_op jit(solution)/shard_map/project_spatial/pallas_call | solution.py:304
  139.4 1.4 project_temporal.1
  140.8 14.3 %all_to_all.20.blocks = bf16[4,192,768]{2,1,0:T(8,128)(2,1)S(1)} all-to-all(bf16[4,192,768]{2,1,0:T(8,128)(2,1)S(1)} %project_temporal.1), channel_id=1, replica_groups=mesh['z'=8,'x'=4,'y'=4,'core'=2] {'y'}, dimensions={0} | all-to-all | bytes 2359296 | tf_op jit(solution)/shard_map/all_to_all | solution.py:423
  155.1 1.1 finish.1
  (24 shorter events, 0.1 us)
Async XLA Ops:
  1.6 10.3 %all-to-all-start = ((bf16[8,12,384]{2,1,0:T(8,128)(2,1)}), bf16[8,12,384]{2,1,0:T(8,128)(2,1)S(1)}, u32[]{:S(2)}, u32[]{:S(2)}) async-start(bf16[8,12,384]{2,1,0:T(8,128)(2,1)} %bitcast.8), calls=%async_computation | async-start | bytes 196608 | tf_op jit(solution)/shard_map/all_to_all | solution.py:377
  11.8 71.7 %all-to-all-start.1 = ((bf16[32,3,48,128]{3,2,1,0:T(8,128)(2,1)}), bf16[32,3,48,128]{3,2,1,0:T(8,128)(2,1)S(1)}, u32[]{:S(2)}, u32[]{:S(2)}) async-start(bf16[32,3,48,128]{3,2,1,0:T(8,128)(2,1)} %pack_temporal.1), calls=%async_computation.1 | async-start | bytes 2359296 | tf_op jit(solution)/shard_map/all_to_all | solution.py:383
  28.0 9.5 %collective-permute-start = (bf16[3,2,192,128]{3,2,1,0:T(8,128)(2,1)}, bf16[3,2,192,128]{3,2,1,0:T(8,128)(2,1)S(1)}, u32[]{:S(2)}, u32[]{:S(2)}) collective-permute-start(bf16[3,2,192,128]{3,2,1,0:T(8,128)(2,1)} %get-tuple-element.19), channel_id=1, source_target_pairs={{0,2},{2,4},{4,6},{6,0},{1,3},{3,5},{5,7},{7,1},{8,10},{10,12},{12... | collective-permute-start | bytes 884744 | tf_op jit(solution)/shard_map/ppermute | solution.py:363
  28.6 12.3 %collective-permute-start.10 = (bf16[3,2,192,128]{3,2,1,0:T(8,128)(2,1)}, bf16[3,2,192,128]{3,2,1,0:T(8,128)(2,1)S(1)}, u32[]{:S(2)}, u32[]{:S(2)}) collective-permute-start(bf16[3,2,192,128]{3,2,1,0:T(8,128)(2,1)} %get-tuple-element.25), channel_id=1, source_target_pairs={{0,6},{2,0},{4,2},{6,4},{1,7},{3,1},{5,3},{7,5},{8,14},{10,8},{12,... | collective-permute-start | bytes 884744 | tf_op jit(solution)/shard_map/ppermute | solution.py:363
  31.3 11.9 %collective-permute-start.12 = (bf16[3,2,192,128]{3,2,1,0:T(8,128)(2,1)}, bf16[3,2,192,128]{3,2,1,0:T(8,128)(2,1)S(1)}, u32[]{:S(2)}, u32[]{:S(2)}) collective-permute-start(bf16[3,2,192,128]{3,2,1,0:T(8,128)(2,1)} %get-tuple-element.26), channel_id=1, source_target_pairs={{0,7},{1,6},{2,1},{3,0},{4,3},{5,2},{6,5},{7,4},{8,15},{9,14},{10,... | collective-permute-start | bytes 884744 | tf_op jit(solution)/shard_map/ppermute | solution.py:372
  37.5 15.6 %collective-permute-start.3 = (bf16[3,2,192,128]{3,2,1,0:T(8,128)(2,1)S(1)}, bf16[3,2,192,128]{3,2,1,0:T(8,128)(2,1)S(1)}, u32[]{:S(2)}, u32[]{:S(2)}) collective-permute-start(bf16[3,2,192,128]{3,2,1,0:T(8,128)(2,1)S(1)} %collective-permute-done.refs_1_), channel_id=1, source_target_pairs={{0,2},{2,4},{4,6},{6,0},{1,3},{3,5},{5,7},{7,1},{8,10},{10,12},{12... | collective-permute-start | bytes 884744 | tf_op jit(solution)/shard_map/ppermute | solution.py:363
  37.6 14.8 %collective-permute-start.1 = (bf16[96,384]{1,0:T(8,128)(2,1)S(1)}, bf16[96,384]{1,0:T(8,128)(2,1)S(1)}, u32[]{:S(2)}, u32[]{:S(2)}) collective-permute-start(bf16[96,384]{1,0:T(8,128)(2,1)S(1)} %after.1.second), channel_id=1, source_target_pairs={{0,32},{32,64},{64,96},{96,128},{128,160},{160,192},{192,224},{224... | collective-permute-start | bytes 221192 | tf_op jit(solution)/shard_map/ppermute | solution.py:363
  39.1 13.2 %collective-permute-start.2 = (bf16[96,384]{1,0:T(8,128)(2,1)S(1)}, bf16[96,384]{1,0:T(8,128)(2,1)S(1)}, u32[]{:S(2)}, u32[]{:S(2)}) collective-permute-start(bf16[96,384]{1,0:T(8,128)(2,1)S(1)} %after.1.second), channel_id=1, source_target_pairs={{0,224},{32,0},{64,32},{96,64},{128,96},{160,128},{192,160},{224,1... | collective-permute-start | bytes 221192 | tf_op jit(solution)/shard_map/ppermute | solution.py:363
  40.9 14.5 %collective-permute-start.6 = (bf16[3,2,192,128]{3,2,1,0:T(8,128)(2,1)}, bf16[3,2,192,128]{3,2,1,0:T(8,128)(2,1)S(1)}, u32[]{:S(2)}, u32[]{:S(2)}) collective-permute-start(bf16[3,2,192,128]{3,2,1,0:T(8,128)(2,1)} %get-tuple-element.21), channel_id=1, source_target_pairs={{0,2},{2,4},{4,6},{6,0},{1,3},{3,5},{5,7},{7,1},{8,10},{10,12},{12... | collective-permute-start | bytes 884744 | tf_op jit(solution)/shard_map/ppermute | solution.py:363
  43.2 16.2 %collective-permute-start.7 = (bf16[3,2,192,128]{3,2,1,0:T(8,128)(2,1)}, bf16[3,2,192,128]{3,2,1,0:T(8,128)(2,1)S(1)}, u32[]{:S(2)}, u32[]{:S(2)}) collective-permute-start(bf16[3,2,192,128]{3,2,1,0:T(8,128)(2,1)} %get-tuple-element.22), channel_id=1, source_target_pairs={{0,6},{2,0},{4,2},{6,4},{1,7},{3,1},{5,3},{7,5},{8,14},{10,8},{12,... | collective-permute-start | bytes 884744 | tf_op jit(solution)/shard_map/ppermute | solution.py:363
  52.4 8.1 %collective-permute-start.8 = (bf16[3,2,192,128]{3,2,1,0:T(8,128)(2,1)}, bf16[3,2,192,128]{3,2,1,0:T(8,128)(2,1)S(1)}, u32[]{:S(2)}, u32[]{:S(2)}) collective-permute-start(bf16[3,2,192,128]{3,2,1,0:T(8,128)(2,1)} %get-tuple-element.23), channel_id=1, source_target_pairs={{0,1},{1,0},{2,3},{3,2},{4,5},{5,4},{6,7},{7,6},{8,9},{9,8},{10,11... | collective-permute-start | bytes 884744 | tf_op jit(solution)/shard_map/ppermute | solution.py:363
  52.4 10.1 %collective-permute-start.9 = (bf16[3,2,192,128]{3,2,1,0:T(8,128)(2,1)}, bf16[3,2,192,128]{3,2,1,0:T(8,128)(2,1)S(1)}, u32[]{:S(2)}, u32[]{:S(2)}) collective-permute-start(bf16[3,2,192,128]{3,2,1,0:T(8,128)(2,1)} %get-tuple-element.24), channel_id=1, source_target_pairs={{0,3},{1,2},{2,5},{3,4},{4,7},{5,6},{6,1},{7,0},{8,11},{9,10},{10,... | collective-permute-start | bytes 884744 | tf_op jit(solution)/shard_map/ppermute | solution.py:372
  53.1 9.4 %collective-permute-start.11 = (bf16[3,2,192,128]{3,2,1,0:T(8,128)(2,1)S(1)}, bf16[3,2,192,128]{3,2,1,0:T(8,128)(2,1)S(1)}, u32[]{:S(2)}, u32[]{:S(2)}) collective-permute-start(bf16[3,2,192,128]{3,2,1,0:T(8,128)(2,1)S(1)} %collective-permute-done.10), channel_id=1, source_target_pairs={{0,7},{1,6},{2,1},{3,0},{4,3},{5,2},{6,5},{7,4},{8,15},{9,14},{10,... | collective-permute-start | bytes 884744 | tf_op jit(solution)/shard_map/ppermute | solution.py:372
  55.4 19.4 %collective-permute-start.4 = (bf16[3,96,384]{2,1,0:T(8,128)(2,1)S(1)}, bf16[3,96,384]{2,1,0:T(8,128)(2,1)S(1)}, u32[]{:S(2)}, u32[]{:S(2)}) collective-permute-start(bf16[3,96,384]{2,1,0:T(8,128)(2,1)S(1)} %join3.1.near), channel_id=1, source_target_pairs={{0,96},{32,128},{64,160},{96,192},{128,224},{160,0},{192,32},{224,... | collective-permute-start | bytes 663560 | tf_op jit(solution)/shard_map/ppermute | solution.py:363
  59.4 15.3 %collective-permute-start.5 = (bf16[3,96,384]{2,1,0:T(8,128)(2,1)S(1)}, bf16[3,96,384]{2,1,0:T(8,128)(2,1)S(1)}, u32[]{:S(2)}, u32[]{:S(2)}) collective-permute-start(bf16[3,96,384]{2,1,0:T(8,128)(2,1)S(1)} %join3.1.near), channel_id=1, source_target_pairs={{0,160},{32,192},{64,224},{96,0},{128,32},{160,64},{192,96},{224,1... | collective-permute-start | bytes 663560 | tf_op jit(solution)/shard_map/ppermute | solution.py:363
  62.5 1.0 copy-start.1
  70.1 13.4 %collective-permute-start.18 = (bf16[4,192,256]{2,1,0:T(8,128)(2,1)}, bf16[4,192,256]{2,1,0:T(8,128)(2,1)}, u32[]{:S(2)}, u32[]{:S(2)}) collective-permute-start(bf16[4,192,256]{2,1,0:T(8,128)(2,1)} %get-tuple-element.27._.refs_0_), channel_id=1, source_target_pairs={{0,2},{2,4},{4,6},{6,0},{1,3},{3,5},{5,7},{7,1},{8,10},{10,12},{12... | collective-permute-start | bytes 1179656 | tf_op jit(solution)/shard_map/ppermute | solution.py:363
  74.8 19.6 %collective-permute-start.13 = (bf16[8,96,384]{2,1,0:T(8,128)(2,1)S(1)}, bf16[8,96,384]{2,1,0:T(8,128)(2,1)S(1)}, u32[]{:S(2)}, u32[]{:S(2)}) collective-permute-start(bf16[8,96,384]{2,1,0:T(8,128)(2,1)S(1)} %join8.1.own), channel_id=1, source_target_pairs={{0,8},{8,16},{16,24},{24,0},{1,9},{9,17},{17,25},{25,1},{2,10},{10... | collective-permute-start | bytes 1769480 | tf_op jit(solution)/shard_map/ppermute | solution.py:363
  76.5 19.7 %collective-permute-start.17 = (bf16[4,192,256]{2,1,0:T(8,128)(2,1)S(1)}, bf16[4,192,256]{2,1,0:T(8,128)(2,1)}, u32[]{:S(2)}, u32[]{:S(2)}) collective-permute-start(bf16[4,192,256]{2,1,0:T(8,128)(2,1)S(1)} %get-tuple-element.28), channel_id=1, source_target_pairs={{0,1},{1,0},{2,3},{3,2},{4,5},{5,4},{6,7},{7,6},{8,9},{9,8},{10,11... | collective-permute-start | bytes 1179656 | tf_op jit(solution)/shard_map/ppermute | solution.py:363
  85.6 28.8 %all-to-all-start.2 = ((bf16[32,48,128]{2,1,0:T(8,128)(2,1)}), bf16[32,48,128]{2,1,0:T(8,128)(2,1)}, u32[]{:S(2)}, u32[]{:S(2)}) async-start(bf16[32,48,128]{2,1,0:T(8,128)(2,1)} %temporal.1), calls=%async_computation.2 | async-start | bytes 786432 | tf_op jit(solution)/shard_map/all_to_all | solution.py:413
  94.1 18.7 %collective-permute-start.15 = (bf16[8,96,384]{2,1,0:T(8,128)(2,1)S(1)}, bf16[8,96,384]{2,1,0:T(8,128)(2,1)S(1)}, u32[]{:S(2)}, u32[]{:S(2)}) collective-permute-start(bf16[8,96,384]{2,1,0:T(8,128)(2,1)S(1)} %join8.1.own), channel_id=1, source_target_pairs={{0,24},{8,0},{16,8},{24,16},{1,25},{9,1},{17,9},{25,17},{2,26},{10... | collective-permute-start | bytes 1769480 | tf_op jit(solution)/shard_map/ppermute | solution.py:363
  94.4 19.7 %collective-permute-start.14 = (bf16[8,96,384]{2,1,0:T(8,128)(2,1)S(1)}, bf16[8,96,384]{2,1,0:T(8,128)(2,1)S(1)}, u32[]{:S(2)}, u32[]{:S(2)}) collective-permute-start(bf16[8,96,384]{2,1,0:T(8,128)(2,1)S(1)} %collective-permute-done.13.behind), channel_id=1, source_target_pairs={{0,8},{8,16},{16,24},{24,0},{1,9},{9,17},{17,25},{25,1},{2,10},{10... | collective-permute-start | bytes 1769480 | tf_op jit(solution)/shard_map/ppermute | solution.py:363
  96.2 12.4 %collective-permute-start.21 = (bf16[4,192,256]{2,1,0:T(8,128)(2,1)}, bf16[4,192,256]{2,1,0:T(8,128)(2,1)}, u32[]{:S(2)}, u32[]{:S(2)}) collective-permute-start(bf16[4,192,256]{2,1,0:T(8,128)(2,1)} %collective-permute-done.17.refs_1_), channel_id=1, source_target_pairs={{0,6},{2,0},{4,2},{6,4},{1,7},{3,1},{5,3},{7,5},{8,14},{10,8},{12,... | collective-permute-start | bytes 1179656 | tf_op jit(solution)/shard_map/ppermute | solution.py:363
  97.9 17.6 %collective-permute-start.23 = (bf16[4,192,256]{2,1,0:T(8,128)(2,1)}, bf16[4,192,256]{2,1,0:T(8,128)(2,1)}, u32[]{:S(2)}, u32[]{:S(2)}) collective-permute-start(bf16[4,192,256]{2,1,0:T(8,128)(2,1)} %get-tuple-element.27._.refs_0_), channel_id=1, source_target_pairs={{0,6},{2,0},{4,2},{6,4},{1,7},{3,1},{5,3},{7,5},{8,14},{10,8},{12,... | collective-permute-start | bytes 1179656 | tf_op jit(solution)/shard_map/ppermute | solution.py:363
  98.0 18.3 %collective-permute-start.20 = (bf16[4,192,256]{2,1,0:T(8,128)(2,1)}, bf16[4,192,256]{2,1,0:T(8,128)(2,1)}, u32[]{:S(2)}, u32[]{:S(2)}) collective-permute-start(bf16[4,192,256]{2,1,0:T(8,128)(2,1)} %collective-permute-done.18.refs_2_._), channel_id=1, source_target_pairs={{0,2},{2,4},{4,6},{6,0},{1,3},{3,5},{5,7},{7,1},{8,10},{10,12},{12... | collective-permute-start | bytes 1179656 | tf_op jit(solution)/shard_map/ppermute | solution.py:363
  108.5 10.3 %collective-permute-start.19 = (bf16[4,192,256]{2,1,0:T(8,128)(2,1)}, bf16[4,192,256]{2,1,0:T(8,128)(2,1)}, u32[]{:S(2)}, u32[]{:S(2)}) collective-permute-start(bf16[4,192,256]{2,1,0:T(8,128)(2,1)} %collective-permute-done.17.refs_1_), channel_id=1, source_target_pairs={{0,2},{2,4},{4,6},{6,0},{1,3},{3,5},{5,7},{7,1},{8,10},{10,12},{12... | collective-permute-start | bytes 1179656 | tf_op jit(solution)/shard_map/ppermute | solution.py:363
  112.7 12.4 %collective-permute-start.22 = (bf16[4,192,256]{2,1,0:T(8,128)(2,1)}, bf16[4,192,256]{2,1,0:T(8,128)(2,1)}, u32[]{:S(2)}, u32[]{:S(2)}) collective-permute-start(bf16[4,192,256]{2,1,0:T(8,128)(2,1)} %collective-permute-done.21.refs_7_), channel_id=1, source_target_pairs={{0,6},{2,0},{4,2},{6,4},{1,7},{3,1},{5,3},{7,5},{8,14},{10,8},{12,... | collective-permute-start | bytes 1179656 | tf_op jit(solution)/shard_map/ppermute | solution.py:363
  114.4 19.5 %collective-permute-start.16 = (bf16[3072,384]{1,0:T(8,128)(2,1)S(1)}, bf16[3072,384]{1,0:T(8,128)(2,1)}, u32[]{:S(2)}, u32[]{:S(2)}) collective-permute-start(bf16[3072,384]{1,0:T(8,128)(2,1)S(1)} %bitcast.9), channel_id=1, source_target_pairs={{0,1},{1,0},{2,3},{3,2},{4,5},{5,4},{6,7},{7,6},{8,9},{9,8},{10,11... | collective-permute-start | bytes 7077896 | tf_op jit(solution)/shard_map/ppermute | solution.py:363
  115.5 15.1 %collective-permute-start.24 = (bf16[16,48,128]{2,1,0:T(8,128)(2,1)S(1)}, bf16[16,48,128]{2,1,0:T(8,128)(2,1)S(1)}, u32[]{:S(2)}, u32[]{:S(2)}) collective-permute-start(bf16[16,48,128]{2,1,0:T(8,128)(2,1)S(1)} %get-tuple-element.31.refs_0_), channel_id=1, source_target_pairs={{0,2},{2,4},{4,6},{6,0},{1,3},{3,5},{5,7},{7,1},{8,10},{10,12},{12... | collective-permute-start | bytes 589832 | tf_op jit(solution)/shard_map/ppermute | solution.py:363
  116.2 17.7 %copy-start = (s32[24]{0:T(128)S(1)}, s32[24]{0:T(128)}, u32[]{:S(2)}) copy-start(s32[24]{0:T(128)} %kinds.5) | copy-start | bytes 292
  116.2 14.5 %collective-permute-start.27 = (bf16[16,48,128]{2,1,0:T(8,128)(2,1)S(1)}, bf16[16,48,128]{2,1,0:T(8,128)(2,1)S(1)}, u32[]{:S(2)}, u32[]{:S(2)}) collective-permute-start(bf16[16,48,128]{2,1,0:T(8,128)(2,1)S(1)} %get-tuple-element.32.refs_1_), channel_id=1, source_target_pairs={{0,6},{2,0},{4,2},{6,4},{1,7},{3,1},{5,3},{7,5},{8,14},{10,8},{12,... | collective-permute-start | bytes 589832 | tf_op jit(solution)/shard_map/ppermute | solution.py:363
  127.3 12.0 %collective-permute-start.25 = (bf16[16,48,128]{2,1,0:T(8,128)(2,1)S(1)}, bf16[16,48,128]{2,1,0:T(8,128)(2,1)S(1)}, u32[]{:S(2)}, u32[]{:S(2)}) collective-permute-start(bf16[16,48,128]{2,1,0:T(8,128)(2,1)S(1)} %get-tuple-element.32.refs_1_), channel_id=1, source_target_pairs={{0,2},{2,4},{4,6},{6,0},{1,3},{3,5},{5,7},{7,1},{8,10},{10,12},{12... | collective-permute-start | bytes 589832 | tf_op jit(solution)/shard_map/ppermute | solution.py:363
  127.4 11.9 %collective-permute-start.29 = (bf16[16,48,128]{2,1,0:T(8,128)(2,1)S(1)}, bf16[16,48,128]{2,1,0:T(8,128)(2,1)S(1)}, u32[]{:S(2)}, u32[]{:S(2)}) collective-permute-start(bf16[16,48,128]{2,1,0:T(8,128)(2,1)S(1)} %get-tuple-element.31.refs_0_), channel_id=1, source_target_pairs={{0,6},{2,0},{4,2},{6,4},{1,7},{3,1},{5,3},{7,5},{8,14},{10,8},{12,... | collective-permute-start | bytes 589832 | tf_op jit(solution)/shard_map/ppermute | solution.py:363
  130.7 8.7 %collective-permute-start.26 = (bf16[16,48,128]{2,1,0:T(8,128)(2,1)S(1)}, bf16[16,48,128]{2,1,0:T(8,128)(2,1)S(1)}, u32[]{:S(2)}, u32[]{:S(2)}) collective-permute-start(bf16[16,48,128]{2,1,0:T(8,128)(2,1)S(1)} %collective-permute-done.24.refs_2_), channel_id=1, source_target_pairs={{0,2},{2,4},{4,6},{6,0},{1,3},{3,5},{5,7},{7,1},{8,10},{10,12},{12... | collective-permute-start | bytes 589832 | tf_op jit(solution)/shard_map/ppermute | solution.py:363
  130.7 8.7 %collective-permute-start.28 = (bf16[16,48,128]{2,1,0:T(8,128)(2,1)S(1)}, bf16[16,48,128]{2,1,0:T(8,128)(2,1)S(1)}, u32[]{:S(2)}, u32[]{:S(2)}) collective-permute-start(bf16[16,48,128]{2,1,0:T(8,128)(2,1)S(1)} %collective-permute-done.27.refs_7_), channel_id=1, source_target_pairs={{0,6},{2,0},{4,2},{6,4},{1,7},{3,1},{5,3},{7,5},{8,14},{10,8},{12,... | collective-permute-start | bytes 589832 | tf_op jit(solution)/shard_map/ppermute | solution.py:363
